TPU v7x, 256 devices: a whole 4x4x8 slice. The times are simulated.
256 devices in a mesh: pipe: 4 (over y_hi, core), head: 16 (over z, y_lo), dp: 4 (over x).
Axes of the slice: x: 4, y: 4 (y_hi: 2, y_lo: 2; y = y_hi * 2 + y_lo), z: 8, core: 2. Of those that a mesh axis runs over, the one named last changes fastest.
Arguments:
- fwd_qkv: bfloat16 [4, 4, 1024, 3, 4096], P('dp', 'pipe', 'head'), may hold values from -6 to 6
- bwd_qkv: bfloat16 [4, 4, 1024, 3, 4096], P('dp', 'pipe', 'head'), may hold values from -6 to 6
- bwd_grad_out: bfloat16 [4, 4, 1024, 4096], P('dp', 'pipe', 'head'), may hold values from -6 to 6
- fwd_doc: int32 [4, 4, 1024], P('dp', 'pipe'), may hold values from 0 to 3, never falling along the last dimension, each value on 1 to 512 neighbouring positions
- bwd_doc: int32 [4, 4, 1024], P('dp', 'pipe'), may hold values from 0 to 3, never falling along the last dimension, each value on 1 to 512 neighbouring positions
- norm_gain: float32 [4, 2, 32, 128], replicated, may hold values from 0.6 to 5.5
- grad_acc: float32 [4, 4, 2, 2, 32, 128], P('dp', 'pipe', None, None, 'head'), may hold values from -96 to 96
Outputs:
- fwd_out: bfloat16 [4, 4, 1024, 4096], P('dp', 'pipe', 'head')
- bwd_qkv_grad: bfloat16 [4, 4, 1024, 3, 4096], P('dp', 'pipe', 'head')
- gain_grad: float32 [4, 2, 32, 128], P('pipe', None, 'head')
Inputs may be any that keep to these rules, and one draw needn't show every extreme that they name: `fwd_doc`: document ids never fall along a sequence. `bwd_doc`: document ids never fall along a sequence.
All inputs are finite; a program needn't handle non-finite values.
Results may differ from a plain program's by a relative error of at most 0.013.
The roundings to bfloat16 on the way count: a program that leaves them out, or rounds other values in their place, can miss the bound.
Values may be sent and summed in bfloat16 or wider, within the bound.
No kernel may reach another device: no remote copies, remote signals or barrier semaphores. Data moves between devices by JAX's collectives and lax.ppermute only.
A program may use at most 64 MiB of HBM per device.

v0:
```python
import math

import jax
import jax.numpy as jnp
from jax import lax
from jax.sharding import PartitionSpec as P

EPS = 1e-06


def swapped(value, axis, stride):
    mask = 2**stride
    pairs = [(source, source ^ mask) for source in range(lax.axis_size(axis))]
    return lax.ppermute(value, axis, pairs)


def normalize(raw, gain):
    values = raw.astype(jnp.float32)
    recip = lax.rsqrt(jnp.mean(values * values, axis=-1, keepdims=True) + EPS)
    unit = values * recip
    return (unit, recip, (unit * gain).astype(jnp.bfloat16))


def block_probs(queries, keys, doc_rows, doc_cols, start):
    scale = 1.0 / math.sqrt(queries.shape[-1])
    scores = jnp.einsum("qhd,khd->hqk", queries, keys, preferred_element_type=jnp.float32) * scale
    rows = start + jnp.arange(queries.shape[0], dtype=jnp.int32)
    cols = jnp.arange(keys.shape[0], dtype=jnp.int32)
    allowed = (cols[None, :] <= rows[:, None]) & (doc_cols[None, :] == doc_rows[:, None])
    scores = jnp.where(allowed[None], scores, -jnp.inf)
    peak = jnp.max(scores, axis=-1, keepdims=True)
    expo = jnp.exp(scores - peak)
    return expo / jnp.sum(expo, axis=-1, keepdims=True)


def forward_heads(queries, keys, values, docs):
    length = queries.shape[0]
    block_rows = min(512, length)
    pieces = []
    for block in range(length // block_rows):
        start = block * block_rows
        finish = start + block_rows
        probs = block_probs(
            queries[start:finish], keys[:finish], docs[start:finish], docs[:finish], start
        ).astype(jnp.bfloat16)
        result = jnp.einsum(
            "hqk,khd->qhd", probs, values[:finish], preferred_element_type=jnp.float32
        )
        pieces.append(result.astype(jnp.bfloat16))
    return jnp.concatenate(pieces, axis=0)


def backward_heads(queries, keys, values, upstream_all, docs):
    length = queries.shape[0]
    block_rows = min(512, length)
    scale = 1.0 / math.sqrt(queries.shape[-1])
    key_grad = jnp.zeros(queries.shape, jnp.float32)
    value_grad = jnp.zeros(queries.shape, jnp.float32)
    query_parts = []
    for block in range(length // block_rows):
        start = block * block_rows
        finish = start + block_rows
        probs = block_probs(
            queries[start:finish], keys[:finish], docs[start:finish], docs[:finish], start
        )
        rounded = probs.astype(jnp.bfloat16)
        outputs = jnp.einsum(
            "hqk,khd->qhd", rounded, values[:finish], preferred_element_type=jnp.float32
        )
        upstream = upstream_all[start:finish]
        dsum = jnp.sum(upstream.astype(jnp.float32) * outputs, axis=-1)
        dprob = jnp.einsum(
            "qhd,khd->hqk", upstream, values[:finish], preferred_element_type=jnp.float32
        )
        dscore = (probs * (dprob - dsum.T[:, :, None])).astype(jnp.bfloat16)
        query_parts.append(
            (
                jnp.einsum(
                    "hqk,khd->qhd", dscore, keys[:finish], preferred_element_type=jnp.float32
                )
                * scale
            ).astype(jnp.bfloat16)
        )
        key_grad = key_grad.at[:finish].add(
            jnp.einsum(
                "hqk,qhd->khd", dscore, queries[start:finish], preferred_element_type=jnp.float32
            )
            * scale
        )
        value_grad = value_grad.at[:finish].add(
            jnp.einsum("hqk,qhd->khd", rounded, upstream, preferred_element_type=jnp.float32)
        )
    return (
        jnp.concatenate(query_parts, axis=0),
        key_grad.astype(jnp.bfloat16),
        value_grad.astype(jnp.bfloat16),
    )


def norm_back(grad_normed, unit, recip, gain):
    normed = grad_normed.astype(jnp.float32)
    scaled = normed * gain
    grad_in = recip * (scaled - unit * jnp.mean(scaled * unit, axis=-1, keepdims=True))
    return (grad_in.astype(jnp.bfloat16), jnp.sum(normed * unit, axis=0))


def mirrored(values, pipe_count):
    moved = values
    for bit in range(pipe_count.bit_length() - 1):
        moved = swapped(moved, "pipe", bit)
    return moved


def body(fwd_qkv, bwd_qkv, bwd_grad_out, fwd_doc, bwd_doc, norm_gain, grad_acc):
    head_count = lax.axis_size("head")
    pipe_count = lax.axis_size("pipe")
    pipe_at = lax.axis_index("pipe")
    tokens = fwd_qkv.shape[2]
    width = fwd_qkv.shape[4]
    heads = norm_gain.shape[2]
    head_dim = norm_gain.shape[3]
    local_heads = heads // head_count
    gain_down = lax.dynamic_index_in_dim(norm_gain, pipe_at, 0, keepdims=False)
    gain_up = lax.dynamic_index_in_dim(norm_gain, pipe_count - 1 - pipe_at, 0, keepdims=False)
    fwd_docs = fwd_doc.reshape(-1)
    bwd_docs = bwd_doc.reshape(-1)
    fwd_raw = fwd_qkv.reshape(tokens, 3, heads, head_dim)
    fwd_query = normalize(fwd_raw[:, 0], gain_down[0])[2]
    fwd_key = normalize(fwd_raw[:, 1], gain_down[1])[2]
    fwd_pack = jnp.stack([fwd_query, fwd_key, fwd_raw[:, 2]], axis=1).reshape(
        tokens, 3, head_count, local_heads, head_dim
    )
    bwd_raw = bwd_qkv.reshape(tokens, 3, heads, head_dim)
    query_unit, query_recip, bwd_query = normalize(bwd_raw[:, 0], gain_up[0])
    key_unit, key_recip, bwd_key = normalize(bwd_raw[:, 1], gain_up[1])
    bwd_pack = jnp.stack([bwd_query, bwd_key, bwd_raw[:, 2]], axis=1).reshape(
        tokens, 3, head_count, local_heads, head_dim
    )
    grad_pack = bwd_grad_out.reshape(tokens, 1, head_count, local_heads, head_dim)
    group = lax.all_to_all(fwd_pack, "head", split_axis=2, concat_axis=0, tiled=True)
    result = forward_heads(group[:, 0, 0], group[:, 1, 0], group[:, 2, 0], fwd_docs)
    fwd_heads = result[:, None, None]
    fwd_back = lax.all_to_all(fwd_heads, "head", split_axis=0, concat_axis=2, tiled=True)
    packed = lax.all_to_all(bwd_pack, "head", split_axis=2, concat_axis=0, tiled=True)
    upstream = lax.all_to_all(grad_pack, "head", split_axis=2, concat_axis=0, tiled=True)
    query_grad, key_grad, value_grad = backward_heads(
        packed[:, 0, 0], packed[:, 1, 0], packed[:, 2, 0], upstream[:, 0, 0], bwd_docs
    )
    bwd_heads = jnp.stack([query_grad, key_grad, value_grad], axis=1)[:, :, None]
    bwd_back = lax.all_to_all(bwd_heads, "head", split_axis=0, concat_axis=2, tiled=True)
    fwd_out = fwd_back.reshape(1, 1, tokens, width)
    returned = bwd_back.reshape(tokens, 3, heads, head_dim)
    query_in, query_part = norm_back(returned[:, 0], query_unit, query_recip, gain_up[0])
    key_in, key_part = norm_back(returned[:, 1], key_unit, key_recip, gain_up[1])
    qkv_grad = jnp.stack([query_in, key_in, returned[:, 2]], axis=1).reshape(1, 1, tokens, 3, width)
    partial_value = jnp.stack([query_part, key_part])
    up_share = lax.psum_scatter(
        partial_value.astype(jnp.bfloat16), "head", scatter_dimension=1, tiled=True
    ).astype(jnp.float32)
    accum = grad_acc.reshape(2, 2, local_heads, head_dim)
    down_local = accum[0]
    up_local = accum[1] + up_share
    down_summed, up_summed = lax.psum((down_local, up_local), "dp")
    total = down_summed + mirrored(up_summed, pipe_count)
    return (fwd_out, qkv_grad, total.reshape(1, 2, local_heads, head_dim))


def solution(mesh):
    in_specs = (
        P("dp", "pipe", "head", None, None),
        P("dp", "pipe", "head", None, None),
        P("dp", "pipe", "head", None),
        P("dp", "pipe", None),
        P("dp", "pipe", None),
        P(),
        P("dp", "pipe", None, None, "head", None),
    )
    out_specs = (
        P("dp", "pipe", "head", None),
        P("dp", "pipe", "head", None, None),
        P("pipe", None, "head", None),
    )
    return jax.shard_map(body, mesh=mesh, in_specs=in_specs, out_specs=out_specs, check_vma=False)
```

profile of v0, /device:TPU:2, one launch (start us, length us, event | category | flops | bytes accessed | tf_op | source)
XLA Modules:
  0.0 284.9 jit_solution(2383571400725760161)
XLA Ops:
  3.2 9.6 %all-to-all-start.3 = ((bf16[64,1,16,2,128]{4,0,3,1,2:T(8,128)(2,1)}), bf16[64,1,16,2,128]{4,0,3,1,2:T(8,128)(2,1)}, u32[]{:S(2)}, u32[]{:S(2)}) async-start(bf16[64,1,16,2,128]{4,0,3,1,2:T(8,128)(2,1)} %copy.143), calls=%async_computation.3 | async-start | bytes 1048576 | tf_op jit(solution)/shard_map/all_to_all | solution.py:145
  15.6 2.1 copy.140
  17.7 2.4 fusion.53
  22.7 7.3 %all-to-all-done.3 = bf16[64,1,16,2,128]{4,0,3,1,2:T(8,128)(2,1)} async-done(((bf16[64,1,16,2,128]{4,0,3,1,2:T(8,128)(2,1)}), bf16[64,1,16,2,128]{4,0,3,1,2:T(8,128)(2,1)}, u32[]{:S(2)}, u32[]{:S(2)}) %all-to-all-start.3) | async-done | bytes 524320 | tf_op jit(solution)/shard_map/all_to_all | solution.py:145
  30.0 4.4 %all-to-all-start.2 = ((bf16[64,3,16,2,128]{4,0,3,1,2:T(8,128)(2,1)}), bf16[64,3,16,2,128]{4,0,3,1,2:T(8,128)(2,1)}, u32[]{:S(2)}, u32[]{:S(2)}) async-start(bf16[64,3,16,2,128]{4,0,3,1,2:T(8,128)(2,1)} %copy.141), calls=%async_computation.2 | async-start | bytes 3145728 | tf_op jit(solution)/shard_map/all_to_all | solution.py:144
  38.3 34.2 %all-to-all-done.2 = bf16[64,3,16,2,128]{4,0,3,1,2:T(8,128)(2,1)} async-done(((bf16[64,3,16,2,128]{4,0,3,1,2:T(8,128)(2,1)}), bf16[64,3,16,2,128]{4,0,3,1,2:T(8,128)(2,1)}, u32[]{:S(2)}, u32[]{:S(2)}) %all-to-all-start.2) | async-done | bytes 1572896 | tf_op jit(solution)/shard_map/all_to_all | solution.py:144
  72.6 4.6 %all-to-all-start = ((bf16[64,3,16,2,128]{4,0,3,1,2:T(8,128)(2,1)}), bf16[64,3,16,2,128]{4,0,3,1,2:T(8,128)(2,1)}, u32[]{:S(2)}, u32[]{:S(2)}) async-start(bf16[64,3,16,2,128]{4,0,3,1,2:T(8,128)(2,1)} %copy.130), calls=%async_computation | async-start | bytes 3145728 | tf_op jit(solution)/shard_map/all_to_all | solution.py:140
  78.1 1.8 fusion.12
  81.8 1.6 copy.142
  83.3 3.2 %fusion.105 = (f32[2,512]{1,0:T(2,128)S(1)}, f32[2,512,512]{1,2,0:T(8,128)}) fusion(pred[512,512]{0,1:T(8,128)(4,1)} %fusion.77, bf16[1024,3,1,2,128]{4,0,3,2,1:T(8,128)(2,1)S(1)} %bitcast.299), kind=kOutput, calls=%fused_computation.175 | convolution fusion | flops 136315392 | bytes 2887680 | tf_op jit(solution)/shard_map/sub | solution.py:32
  86.5 2.0 fusion.81
  92.0 2.6 fusion.83
  94.6 21.3 %all-to-all-done = bf16[64,3,16,2,128]{4,0,3,1,2:T(8,128)(2,1)} async-done(((bf16[64,3,16,2,128]{4,0,3,1,2:T(8,128)(2,1)}), bf16[64,3,16,2,128]{4,0,3,1,2:T(8,128)(2,1)}, u32[]{:S(2)}, u32[]{:S(2)}) %all-to-all-start) | async-done | bytes 1572896 | tf_op jit(solution)/shard_map/all_to_all | solution.py:140
  115.9 1.5 copy.131
  118.6 2.7 fusion.82
  121.3 2.0 fusion.103
  123.3 3.1 %fusion.51 = bf16[512,2,128]{0,2,1:T(8,128)(2,1)} fusion(f32[2,512]{1,0:T(2,128)S(1)} %fusion.103, bf16[1024,3,1,2,128]{4,0,3,2,1:T(8,128)(2,1)} %bitcast.313, pred[512,512]{0,1:T(8,128)(4,1)} %fusion.78), kind=kOutput, calls=%fused_computation.90 | convolution fusion | flops 271189504 | bytes 1314816 | tf_op jit(solution)/shard_map/hqk,khd->qhd/dot_general | solution.py:46
  126.4 5.6 %fusion.102 = (f32[2,512]{1,0:T(2,128)S(1)}, f32[2,512,1024]{2,1,0:T(8,128)S(1)}) fusion(f32[2,512,1024]{2,1,0:T(8,128)} %fusion.82, pred[512,1024]{1,0:T(8,128)(4,1)} %get-tuple-element.99), kind=kOutput, calls=%fused_computation.172 | output fusion | flops 6292479 | bytes 8916992 | tf_op jit(solution)/shard_map/sub | solution.py:32
  132.0 2.0 fusion.50
  134.9 2.0 copy.135
  136.9 4.5 %all-to-all-start.1 = ((bf16[1024,1,1,2,128]{4,3,2,1,0:T(2,128)(2,1)}), bf16[1024,1,1,2,128]{4,3,2,1,0:T(2,128)(2,1)}, u32[]{:S(2)}, u32[]{:S(2)}) async-start(bf16[1024,1,1,2,128]{4,3,2,1,0:T(2,128)(2,1)} %copy.135), calls=%async_computation.1 | async-start | bytes 1048576 | tf_op jit(solution)/shard_map/all_to_all | solution.py:143
  141.4 5.6 %fusion.104 = (f32[2,512]{1,0:T(2,128)S(1)}, f32[2,512,1024]{2,1,0:T(8,128)S(1)}) fusion(f32[2,512,1024]{2,1,0:T(8,128)} %fusion.83, pred[512,1024]{1,0:T(8,128)(4,1)} %get-tuple-element.98), kind=kOutput, calls=%fused_computation.174 | output fusion | flops 6292479 | bytes 8916992 | tf_op jit(solution)/shard_map/sub | solution.py:32
  153.0 2.9 %copy.161 = bf16[1024,3,1,2,128]{4,3,1,2,0:T(2,128)(2,1)} copy(bf16[1024,3,1,2,128]{0,4,3,1,2:T(8,128)(2,1)S(1)} %maximum_bitcast_fusion) | data formatting | bytes 3145728 | tf_op jit(solution)/shard_map/broadcast_in_dim | solution.py:149
  155.8 1.8 all-to-all-done.1
  157.6 6.1 %all-to-all-start.4 = ((bf16[1024,3,1,2,128]{4,3,1,2,0:T(2,128)(2,1)}), bf16[1024,3,1,2,128]{4,3,1,2,0:T(2,128)(2,1)S(1)}, u32[]{:S(2)}, u32[]{:S(2)}) async-start(bf16[1024,3,1,2,128]{4,3,1,2,0:T(2,128)(2,1)} %copy.161), calls=%async_computation.4 | async-start | bytes 3145728 | tf_op jit(solution)/shard_map/all_to_all | solution.py:150
  167.5 2.2 reshape.458
  169.7 31.3 %all-to-all-done.4 = bf16[1024,3,1,2,128]{4,3,1,2,0:T(2,128)(2,1)S(1)} async-done(((bf16[1024,3,1,2,128]{4,3,1,2,0:T(2,128)(2,1)}), bf16[1024,3,1,2,128]{4,3,1,2,0:T(2,128)(2,1)S(1)}, u32[]{:S(2)}, u32[]{:S(2)}) %all-to-all-start.4) | async-done | bytes 1572896 | tf_op jit(solution)/shard_map/all_to_all | solution.py:150
  202.3 2.9 %fusion.70 = (bf16[32,128]{1,0:T(8,128)(2,1)S(1)}, f32[64,32]{1,0:T(8,128)S(1)}, f32[64,32]{1,0:T(8,128)S(1)}, bf16[32,128]{1,0:T(8,128)(2,1)S(1)}) fusion(f32[64,32]{1,0:T(8,128)S(1)} %add_rsqrt_fusion.1, bf16[64,1,32,128]{3,0,2,1:T(8,128)(2,1)S(1)} %get-tuple-element.82, bf16[64,3,32,128]{3,2,0,1:T(8,128)(2,1)S(1)} %bitcast.294, ...), kind=kLoop, calls=%fused_computation.109 | loop fusion | flops 4182016 | bytes 2179072 | tf_op jit(solution)/shard_map/reduce_sum | solution.py:104
  205.2 60.7 %all-reduce.2 = bf16[2,32,128]{2,1,0:T(8,128)(2,1)S(1)} all-reduce(bf16[2,32,128]{2,1,0:T(8,128)(2,1)S(1)} %pad_maximum_fusion.3), channel_id=2, replica_groups=mesh['pipe'=4,'head'=16,'dp'=4] {'head'}, use_global_device_ids=true, to_apply=%region_19.20.clone | all-reduce | flops 8192 | bytes 32768
  265.9 8.6 %all-reduce.3 = (f32[2,2,128]{2,1,0:T(2,128)S(1)}, f32[2,2,128]{2,1,0:T(2,128)S(1)}) all-reduce(f32[2,2,128]{2,1,0:T(2,128)S(1)} %slice_bitcast_fusion.54, f32[2,2,128]{2,1,0:T(2,128)S(1)} %bitcast_add_fusion), channel_id=1, replica_groups=mesh['pipe'=4,'head'=16,'dp'=4] {'dp'}, use_global_device_ids=true, to_apply=%region_16.17 | all-reduce | flops 1024 | bytes 8192 | tf_op jit(solution)/shard_map/psum | solution.py:163
  274.6 2.4 fusion.56
  279.2 3.0 %collective-permute-start.1 = (f32[2,2,128]{2,1,0:T(2,128)S(1)}, f32[2,2,128]{2,1,0:T(2,128)S(1)}, u32[]{:S(2)}, u32[]{:S(2)}) collective-permute-start(f32[2,2,128]{2,1,0:T(2,128)S(1)} %collective-permute-done), channel_id=1, source_target_pairs={{0,128},{64,192},{128,0},{192,64},{1,129},{65,193},{129,1},{193,65... | collective-permute-start | bytes 6152 | tf_op jit(solution)/shard_map/ppermute | solution.py:14
  (102 shorter events, 35.1 us)
Async XLA Ops:
  0.6 12.2 %copy-start.9 = (bf16[1,1,64,3,4096]{4,2,3,1,0:T(8,128)(2,1)S(1)}, bf16[1,1,64,3,4096]{4,2,3,1,0:T(8,128)(2,1)}, u32[]{:S(2)}) copy-start(bf16[1,1,64,3,4096]{4,2,3,1,0:T(8,128)(2,1)} %param.20) | copy-start | bytes 4718596
  3.2 26.9 %all-to-all-start.3 = ((bf16[64,1,16,2,128]{4,0,3,1,2:T(8,128)(2,1)}), bf16[64,1,16,2,128]{4,0,3,1,2:T(8,128)(2,1)}, u32[]{:S(2)}, u32[]{:S(2)}) async-start(bf16[64,1,16,2,128]{4,0,3,1,2:T(8,128)(2,1)} %copy.143), calls=%async_computation.3 | async-start | bytes 1048576 | tf_op jit(solution)/shard_map/all_to_all | solution.py:145
  12.8 1.8 copy-start.10
  14.6 3.1 %copy-start.14 = (f32[4,2,32,128]{3,2,1,0:T(8,128)S(1)}, f32[4,2,32,128]{3,2,1,0:T(8,128)}, u32[]{:S(2)}) copy-start(f32[4,2,32,128]{3,2,1,0:T(8,128)} %param.24) | copy-start | bytes 393220
  20.2 1.0 copy-start.8
  30.0 42.6 %all-to-all-start.2 = ((bf16[64,3,16,2,128]{4,0,3,1,2:T(8,128)(2,1)}), bf16[64,3,16,2,128]{4,0,3,1,2:T(8,128)(2,1)}, u32[]{:S(2)}, u32[]{:S(2)}) async-start(bf16[64,3,16,2,128]{4,0,3,1,2:T(8,128)(2,1)} %copy.141), calls=%async_computation.2 | async-start | bytes 3145728 | tf_op jit(solution)/shard_map/all_to_all | solution.py:144
  34.4 1.0 copy-start.4
  34.4 1.2 copy-start.3
  36.1 1.3 copy-start.15
  36.1 1.3 copy-start.16
  72.6 43.4 %all-to-all-start = ((bf16[64,3,16,2,128]{4,0,3,1,2:T(8,128)(2,1)}), bf16[64,3,16,2,128]{4,0,3,1,2:T(8,128)(2,1)}, u32[]{:S(2)}, u32[]{:S(2)}) async-start(bf16[64,3,16,2,128]{4,0,3,1,2:T(8,128)(2,1)} %copy.130), calls=%async_computation | async-start | bytes 3145728 | tf_op jit(solution)/shard_map/all_to_all | solution.py:140
  86.5 2.7 copy-start.6
  88.5 1.1 copy-start
  117.5 1.1 copy-start.2
  132.0 2.1 copy-start.13
  136.9 20.7 %all-to-all-start.1 = ((bf16[1024,1,1,2,128]{4,3,2,1,0:T(2,128)(2,1)}), bf16[1024,1,1,2,128]{4,3,2,1,0:T(2,128)(2,1)}, u32[]{:S(2)}, u32[]{:S(2)}) async-start(bf16[1024,1,1,2,128]{4,3,2,1,0:T(2,128)(2,1)} %copy.135), calls=%async_computation.1 | async-start | bytes 1048576 | tf_op jit(solution)/shard_map/all_to_all | solution.py:143
  147.0 1.0 copy-start.12
  149.6 1.0 copy-start.11
  149.6 1.1 copy-start.7
  150.5 1.3 copy-start.1
  155.8 7.9 %copy-start.18 = (u32[256]{0:T(256)S(1)}, u32[256]{0:T(256)}, u32[]{:S(2)}) copy-start(u32[256]{0:T(256)} %constant.162) | copy-start | bytes 3076
  155.8 9.2 %copy-start.17 = (f32[1,1,2,2,2,128]{5,4,3,2,1,0:T(2,128)S(1)}, f32[1,1,2,2,2,128]{5,4,3,2,1,0:T(2,128)}, u32[]{:S(2)}) copy-start(f32[1,1,2,2,2,128]{5,4,3,2,1,0:T(2,128)} %param.25) | copy-start | bytes 12292
  157.6 43.3 %all-to-all-start.4 = ((bf16[1024,3,1,2,128]{4,3,1,2,0:T(2,128)(2,1)}), bf16[1024,3,1,2,128]{4,3,1,2,0:T(2,128)(2,1)S(1)}, u32[]{:S(2)}, u32[]{:S(2)}) async-start(bf16[1024,3,1,2,128]{4,3,1,2,0:T(2,128)(2,1)} %copy.161), calls=%async_computation.4 | async-start | bytes 3145728 | tf_op jit(solution)/shard_map/all_to_all | solution.py:150
  274.5 4.6 %collective-permute-start = (f32[2,2,128]{2,1,0:T(2,128)S(1)}, f32[2,2,128]{2,1,0:T(2,128)S(1)}, u32[]{:S(2)}, u32[]{:S(2)}) collective-permute-start(f32[2,2,128]{2,1,0:T(2,128)S(1)} %get-tuple-element.78), channel_id=1, source_target_pairs={{0,64},{64,0},{128,192},{192,128},{1,65},{65,1},{129,193},{193,129... | collective-permute-start | bytes 6152 | tf_op jit(solution)/shard_map/ppermute | solution.py:14
  277.0 1.7 copy-start.5
  279.2 5.2 %collective-permute-start.1 = (f32[2,2,128]{2,1,0:T(2,128)S(1)}, f32[2,2,128]{2,1,0:T(2,128)S(1)}, u32[]{:S(2)}, u32[]{:S(2)}) collective-permute-start(f32[2,2,128]{2,1,0:T(2,128)S(1)} %collective-permute-done), channel_id=1, source_target_pairs={{0,128},{64,192},{128,0},{192,64},{1,129},{65,193},{129,1},{193,65... | collective-permute-start | bytes 6152 | tf_op jit(solution)/shard_map/ppermute | solution.py:14
where the time goes:
time: 288 us; the launch traced here: 285 us
  waiting for transfers between devices  96.8 us (34%)
  blocking collectives  69.3 us (24%)
  starting transfers between devices  32.2 us (11%)
  local copies, waits for them, and re-layouts  31.9 us (11%)
  other arithmetic  29.7 us (10%)
  matrix products  23 us (8%)
    unnamed x1, blocking collectives  60.7 us
    all_to_all x1, waiting for transfers between devices, body(): lax.all_to_all(bwd_pack, 'head', split_axis=2, concat_axis=0, tiled=True)  34.2 us
    all_to_all x1, waiting for transfers between devices, body(): lax.all_to_all(bwd_heads, 'head', split_axis=0, concat_axis=2, tiled=True)  31.3 us
    all_to_all x1, waiting for transfers between devices, body(): lax.all_to_all(fwd_pack, 'head', split_axis=2, concat_axis=0, tiled=True)  21.3 us
    sub x2, other arithmetic, block_probs(): expo = jnp.exp(scores - peak)  11.2 us
    all_to_all x1, starting transfers between devices, body(): lax.all_to_all(grad_pack, 'head', split_axis=2, concat_axis=0, tiled=True)  9.63 us
    psum x1, blocking collectives, body(): down_summed, up_summed = lax.psum((down_local, up_local), 'dp')  8.59 us
    all_to_all x1, waiting for transfers between devices, body(): lax.all_to_all(grad_pack, 'head', split_axis=2, concat_axis=0, tiled=True)  7.3 us
  transfers between devices with their start and end apart: 7, of which 6 were waited for; matrix products, arithmetic and copies ran while one was open for 19% of the time, Pallas kernels for 0%

commit v1 on v0

v1 whole, which is shorter than its diff:
```python
import functools
import math

import jax
import jax.numpy as jnp
from jax import lax
from jax.experimental import pallas as pl
from jax.experimental.pallas import tpu as pltpu
from jax.sharding import PartitionSpec as P

EPS = 1e-06
LONGEST = 512
BLOCK = 128
NT = (((1,), (1,)), ((), ()))
NN = (((1,), (0,)), ((), ()))
F32 = jnp.float32
BF16 = jnp.bfloat16


def dot(left, right, dims=NN):
    return lax.dot_general(left, right, dims, preferred_element_type=F32)


def unit_of(raw):
    values = raw.astype(F32)
    recip = lax.rsqrt(jnp.mean(values * values, axis=-1, keepdims=True) + EPS)
    return values * recip, recip


def starts_of(docs):
    first = jnp.zeros(docs.shape, jnp.int32)
    for value in range(3):
        count = jnp.sum((docs == value).astype(jnp.int32))
        first = first + jnp.where(docs > value, count, 0)
    return first


def window(block):
    low = max(0, block * BLOCK - LONGEST)
    return low, (block + 1) * BLOCK


def probs_of(keys, query, start, low, high):
    scores = dot(keys, query, NT)
    factor = math.log2(math.e) / math.sqrt(query.shape[-1])
    rows = lax.broadcasted_iota(jnp.int32, (BLOCK, BLOCK), 0)
    cols = lax.broadcasted_iota(jnp.int32, (BLOCK, BLOCK), 1)
    pieces = []
    for at in range(low, high, BLOCK):
        piece = scores[at - low : at - low + BLOCK]
        allowed = rows >= start - at
        if at + BLOCK == high:
            allowed = allowed & (rows <= cols)
        pieces.append(jnp.where(allowed, piece, -1e30))
    peak = jnp.max(functools.reduce(jnp.maximum, pieces), axis=0, keepdims=True)
    pieces = [jnp.exp2((piece - peak) * factor) for piece in pieces]
    total = jnp.sum(functools.reduce(jnp.add, pieces), axis=0, keepdims=True)
    share = 1.0 / total
    return [piece * share for piece in pieces]


def flat(ref, kind, tokens, dim):
    return ref[:, kind].reshape(tokens, dim)


def forward_kernel(raw_ref, gain_ref, doc_ref, _, out_ref, query_ref, key_ref, value_t_ref):
    sources, _, rows, dim = raw_ref.shape
    tokens = sources * rows
    query_ref[...] = (unit_of(flat(raw_ref, 0, tokens, dim))[0] * gain_ref[0]).astype(BF16)
    key_ref[...] = (unit_of(flat(raw_ref, 1, tokens, dim))[0] * gain_ref[1]).astype(BF16)
    value_t_ref[...] = flat(raw_ref, 2, tokens, dim).T
    starts = starts_of(doc_ref[...])
    per = BLOCK // rows
    for block in range(tokens // BLOCK):
        low, high = window(block)
        query = query_ref[block * BLOCK : high]
        probs = probs_of(key_ref[low:high], query, starts[block : block + 1], low, high)
        probs = jnp.concatenate([piece.astype(BF16) for piece in probs], axis=0)
        result = dot(value_t_ref[:, low:high], probs).T.astype(BF16)
        out_ref[block * per : (block + 1) * per, 0] = result.reshape(per, rows, dim)


def norm_back(raw, grad, gain):
    unit, recip = unit_of(raw)
    normed = grad.astype(F32)
    scaled = normed * gain
    grad_in = recip * (scaled - unit * jnp.mean(scaled * unit, axis=-1, keepdims=True))
    return grad_in.astype(BF16), jnp.sum(normed * unit, axis=0, keepdims=True)


def backward_kernel(
    raw_ref, gain_ref, doc_ref, out_ref, new_ref,
    query_ref, key_ref, key_t_ref, value_t_ref, up_t_ref, probs_ref, dscore_ref,
):
    sources, _, rows, dim = raw_ref.shape
    tokens = sources * rows
    scale = 1.0 / math.sqrt(dim)
    query_ref[...] = (unit_of(flat(raw_ref, 0, tokens, dim))[0] * gain_ref[0]).astype(BF16)
    key = (unit_of(flat(raw_ref, 1, tokens, dim))[0] * gain_ref[1]).astype(BF16)
    key_ref[...] = key
    key_t_ref[...] = key.T
    value_t_ref[...] = flat(raw_ref, 2, tokens, dim).T
    up_t_ref[...] = flat(raw_ref, 3, tokens, dim).T
    starts = starts_of(doc_ref[...])
    per = BLOCK // rows
    blocks = tokens // BLOCK
    new_query = jnp.zeros((1, dim), F32)
    new_key = jnp.zeros((1, dim), F32)

    def part(kind, low, high):
        return raw_ref[low // rows : high // rows, kind].reshape(high - low, dim)

    for block in range(blocks):
        low, high = window(block)
        here = slice(block * BLOCK, high)
        query = query_ref[here]
        probs = probs_of(key_ref[low:high], query, starts[block : block + 1], low, high)
        rounded = jnp.concatenate([piece.astype(BF16) for piece in probs], axis=0)
        probs_ref[low:high, here] = rounded
        result_t = dot(value_t_ref[:, low:high], rounded)
        dsum = jnp.sum(up_t_ref[:, here].astype(F32) * result_t, axis=0, keepdims=True)
        dprob = dot(part(2, low, high), part(3, block * BLOCK, high), NT)
        dscore = jnp.concatenate(
            [
                (piece * (dprob[at * BLOCK : (at + 1) * BLOCK] - dsum)).astype(BF16)
                for at, piece in enumerate(probs)
            ],
            axis=0,
        )
        dscore_ref[low:high, here] = dscore
        grad = (dot(key_t_ref[:, low:high], dscore) * scale).T.astype(BF16)
        grad_in, new = norm_back(part(0, block * BLOCK, high), grad, gain_ref[0])
        new_query = new_query + new
        out_ref[block * per : (block + 1) * per, 0] = grad_in.reshape(per, rows, dim)

    for block in range(blocks):
        low = block * BLOCK
        high = min(tokens, low + BLOCK + LONGEST)
        here = slice(low, low + BLOCK)
        grad = (dot(dscore_ref[here, low:high], query_ref[low:high]) * scale).astype(BF16)
        grad_in, new = norm_back(part(1, low, low + BLOCK), grad, gain_ref[1])
        new_key = new_key + new
        out_ref[block * per : (block + 1) * per, 1] = grad_in.reshape(per, rows, dim)
        value_grad = dot(probs_ref[here, low:high], part(3, low, high)).astype(BF16)
        out_ref[block * per : (block + 1) * per, 2] = value_grad.reshape(per, rows, dim)
    new_ref[0] = new_query
    new_ref[1] = new_key


def pack_kernel(*refs):
    out_ref = refs[-1]
    at = 0
    for ref in refs[:-1]:
        kinds = ref.shape[0]
        out_ref[0, at : at + kinds] = ref[...]
        at += kinds


def pack(arrays, ranks):
    rows = arrays[0].shape[1]
    wide = arrays[0].shape[2] // ranks
    kinds = sum(array.shape[0] for array in arrays)
    return pl.pallas_call(
        pack_kernel,
        grid=(ranks,),
        in_specs=[
            pl.BlockSpec((array.shape[0], rows, wide), lambda at: (0, 0, at)) for array in arrays
        ],
        out_specs=pl.BlockSpec((1, kinds, rows, wide), lambda at: (at, 0, 0, 0)),
        out_shape=jax.ShapeDtypeStruct((ranks, kinds, rows, wide), arrays[0].dtype),
        name="pack",
    )(*arrays)


def unpack_kernel(in_ref, bwd_ref, fwd_ref):
    bwd_ref[...] = in_ref[0, 0:3]
    fwd_ref[...] = in_ref[0, 3]


def unpack(array):
    ranks, kinds, rows, wide = array.shape
    return pl.pallas_call(
        unpack_kernel,
        grid=(ranks,),
        in_specs=[pl.BlockSpec((1, kinds, rows, wide), lambda at: (at, 0, 0, 0))],
        out_specs=[
            pl.BlockSpec((kinds - 1, rows, wide), lambda at: (0, 0, at)),
            pl.BlockSpec((rows, wide), lambda at: (0, at)),
        ],
        out_shape=[
            jax.ShapeDtypeStruct((kinds - 1, rows, wide * ranks), array.dtype),
            jax.ShapeDtypeStruct((rows, wide * ranks), array.dtype),
        ],
        name="unpack",
    )(array)


VMEM_LIMIT = 48 * 1024 * 1024


def backward_call(raw, gain, docs):
    ranks, kinds, rows, wide = raw.shape
    dim = gain.shape[-1]
    heads = wide // dim
    tokens = ranks * rows
    return pl.pallas_call(
        backward_kernel,
        grid=(heads,),
        in_specs=[
            pl.BlockSpec((ranks, kinds, rows, dim), lambda at: (0, 0, 0, at)),
            pl.BlockSpec((2, None, 1, dim), lambda at: (0, at, 0, 0)),
            pl.BlockSpec(docs.shape, lambda at: (0, 0)),
        ],
        out_specs=[
            pl.BlockSpec((ranks, 3, rows, dim), lambda at: (0, 0, 0, at)),
            pl.BlockSpec((2, None, 1, dim), lambda at: (0, at, 0, 0)),
        ],
        out_shape=[
            jax.ShapeDtypeStruct((ranks, 4, rows, wide), raw.dtype),
            jax.ShapeDtypeStruct((2, heads, 1, dim), F32),
        ],
        scratch_shapes=[
            pltpu.VMEM((tokens, dim), BF16),
            pltpu.VMEM((tokens, dim), BF16),
            pltpu.VMEM((dim, tokens), BF16),
            pltpu.VMEM((dim, tokens), BF16),
            pltpu.VMEM((dim, tokens), BF16),
            pltpu.VMEM((tokens, tokens), BF16),
            pltpu.VMEM((tokens, tokens), BF16),
        ],
        compiler_params=pltpu.CompilerParams(vmem_limit_bytes=VMEM_LIMIT),
        cost_estimate=pl.CostEstimate(
            flops=12 * heads * tokens * tokens * dim // 2,
            bytes_accessed=heads * tokens * dim * 14,
            transcendentals=heads * tokens * tokens // 2,
        ),
        name="backward",
    )(raw, gain, docs)


def forward_call(raw, gain, docs, out):
    ranks, kinds, rows, wide = raw.shape
    dim = gain.shape[-1]
    heads = wide // dim
    tokens = ranks * rows
    return pl.pallas_call(
        forward_kernel,
        grid=(heads,),
        in_specs=[
            pl.BlockSpec((ranks, kinds, rows, dim), lambda at: (0, 0, 0, at)),
            pl.BlockSpec((2, None, 1, dim), lambda at: (0, at, 0, 0)),
            pl.BlockSpec(docs.shape, lambda at: (0, 0)),
            pl.BlockSpec(memory_space=pl.ANY),
        ],
        out_specs=pl.BlockSpec((ranks, 1, rows, dim), lambda at: (0, 3, 0, at)),
        out_shape=jax.ShapeDtypeStruct(out.shape, out.dtype),
        scratch_shapes=[
            pltpu.VMEM((tokens, dim), BF16),
            pltpu.VMEM((tokens, dim), BF16),
            pltpu.VMEM((dim, tokens), BF16),
        ],
        input_output_aliases={3: 0},
        compiler_params=pltpu.CompilerParams(vmem_limit_bytes=VMEM_LIMIT),
        cost_estimate=pl.CostEstimate(
            flops=4 * heads * tokens * tokens * dim // 2,
            bytes_accessed=heads * tokens * dim * 8,
            transcendentals=heads * tokens * tokens // 2,
        ),
        name="forward",
    )(raw, gain, docs, out)


def exchange(value):
    return lax.all_to_all(value, "head", split_axis=0, concat_axis=0, tiled=True)


def body(fwd_qkv, bwd_qkv, bwd_grad_out, fwd_doc, bwd_doc, norm_gain, grad_acc):
    ranks = lax.axis_size("head")
    pipe_count = lax.axis_size("pipe")
    pipe_at = lax.axis_index("pipe")
    head_at = lax.axis_index("head")
    tokens = fwd_qkv.shape[2]
    width = fwd_qkv.shape[4]
    dim = norm_gain.shape[3]
    local_heads = norm_gain.shape[2] // ranks

    def gain_of(section):
        part = lax.dynamic_slice(
            norm_gain, (section, 0, head_at * local_heads, 0), (1, 2, local_heads, dim)
        )
        return part.reshape(2, local_heads, 1, dim)

    gain_down = gain_of(pipe_at)
    gain_up = gain_of(pipe_count - 1 - pipe_at)
    fwd_docs = fwd_doc.reshape(-1, BLOCK)
    bwd_docs = bwd_doc.reshape(-1, BLOCK)
    fwd_raw = fwd_qkv.reshape(tokens, 3, width).transpose(1, 0, 2)
    bwd_raw = bwd_qkv.reshape(tokens, 3, width).transpose(1, 0, 2)
    upstream = bwd_grad_out.reshape(1, tokens, width)

    bwd_group = exchange(pack([bwd_raw, upstream], ranks))
    fwd_group = exchange(pack([fwd_raw], ranks))
    grads, new = backward_call(bwd_group, gain_up, bwd_docs)
    results = forward_call(fwd_group, gain_down, fwd_docs, grads)
    returned = exchange(results)
    qkv_grad, fwd_out = unpack(returned)

    accum = grad_acc.reshape(2, 2, local_heads, dim)
    up_local = accum[1] + new.reshape(2, local_heads, dim)
    mirrored = lax.ppermute(up_local, "pipe", [(at, pipe_count - 1 - at) for at in range(pipe_count)])
    total = lax.psum(accum[0] + mirrored, "dp")
    return (
        fwd_out.reshape(1, 1, tokens, width),
        qkv_grad.transpose(1, 0, 2).reshape(1, 1, tokens, 3, width),
        total.reshape(1, 2, local_heads, dim),
    )


def solution(mesh):
    in_specs = (
        P("dp", "pipe", "head", None, None),
        P("dp", "pipe", "head", None, None),
        P("dp", "pipe", "head", None),
        P("dp", "pipe", None),
        P("dp", "pipe", None),
        P(),
        P("dp", "pipe", None, None, "head", None),
    )
    out_specs = (
        P("dp", "pipe", "head", None),
        P("dp", "pipe", "head", None, None),
        P("pipe", None, "head", None),
    )
    return jax.shard_map(body, mesh=mesh, in_specs=in_specs, out_specs=out_specs, check_vma=False)
```

time: 288 us -> 184 us (0.64)
  blocking collectives: 69.3 us -> 9.16 us
  Pallas kernels: 0 us -> 43.3 us
  other arithmetic: 29.7 us -> 0.01 us
  local copies, waits for them, and re-layouts: 31.9 us -> 3.66 us
  matrix products: 23 us -> 0 us
  starting transfers between devices: 32.2 us -> 18.9 us
  waiting for transfers between devices: 96.8 us -> 107 us
    unnamed x1 -> x0, blocking collectives: 60.7 us -> none
    pallas_call x0 -> x5, Pallas kernels: none -> 43.3 us  [the longest x2 18.7 us: pack(): pl.pallas_call(pack_kernel, grid=(ranks,), in_specs=[pl.BlockSpec((array....]
    dot_general x14 -> x0, matrix products: 17.8 us -> none  [the longest x2 5.31 us: block_probs(): jnp.einsum('qhd,khd->hqk', queries, keys, preferred_element_type=jnp.floa...]
    all_to_all x5 -> x3, starting transfers between devices: 29.2 us -> 17.9 us  [exchange(): lax.all_to_all(value, 'head', split_axis=0, concat_axis=0, tiled=True)]
    sub x2 -> x0, other arithmetic: 11.2 us -> none  [block_probs(): expo = jnp.exp(scores - peak)]
    all_to_all x5 -> x3, waiting for transfers between devices: 95.9 us -> 104 us  [exchange(): lax.all_to_all(value, 'head', split_axis=0, concat_axis=0, tiled=True)]
    convert_element_type x4 -> x0, other arithmetic: 7.39 us -> none  [the longest x2 2.57 us: backward_heads(): rounded = probs.astype(jnp.bfloat16)]
    slice x11 -> x0, local copies, waits for them, and re-layouts: 7.33 us -> none  [the longest x2 2.89 us: body(): bwd_raw[:, 2]]
  transfers between devices with their start and end apart: 7 -> 4, of which waited for: 6 -> 4; matrix products, arithmetic and copies ran while one was open for 19% -> 0% of each run, Pallas kernels for 0% -> 11%
where the time goes in v1:
time: 184 us; the launch traced here: 183 us
  waiting for transfers between devices  107 us (58%)
  Pallas kernels  43.3 us (24%)
  starting transfers between devices  18.9 us (10%)
  blocking collectives  9.16 us (5%)
  local copies, waits for them, and re-layouts  3.66 us (2%)
    all_to_all x3, waiting for transfers between devices, exchange(): lax.all_to_all(value, 'head', split_axis=0, concat_axis=0, tiled=True)  104 us
    pallas_call x2, Pallas kernels, pack(): pl.pallas_call(pack_kernel, grid=(ranks,), in_specs=[pl.BlockSpec((array....  18.7 us
    all_to_all x3, starting transfers between devices, exchange(): lax.all_to_all(value, 'head', split_axis=0, concat_axis=0, tiled=True)  17.9 us
    pallas_call x1, Pallas kernels, backward_call(): pl.pallas_call(backward_kernel, grid=(heads,), in_specs=[pl.BlockSpec((ra...  10.4 us
    pallas_call x1, Pallas kernels, unpack(): pl.pallas_call(unpack_kernel, grid=(ranks,), in_specs=[pl.BlockSpec((1, k...  9.42 us
    psum x1, blocking collectives, body(): total = lax.psum(accum[0] + mirrored, 'dp')  9.16 us
    pallas_call x1, Pallas kernels, forward_call(): pl.pallas_call(forward_kernel, grid=(heads,), in_specs=[pl.BlockSpec((ran...  4.82 us
  transfers between devices with their start and end apart: 4, of which 4 were waited for; matrix products, arithmetic and copies ran while one was open for 0% of the time, Pallas kernels for 11%

profile of v1, /device:TPU:2, one launch (start us, length us, event | category | flops | bytes accessed | tf_op | source)
XLA Modules:
  0.0 182.9 jit_solution(889270964198130953)
XLA Ops:
  0.6 9.4 %pack.3 = bf16[16,4,64,256]{3,2,1,0:T(8,128)(2,1)} custom-call(bf16[3,64,4096]{2,1,0:T(8,128)(2,1)} %bitcast.30, bf16[1,64,4096]{2,1,0:T(8,128)(2,1)} %bitcast.31), custom_call_target="tpu_custom_call" | custom-call | tf_op jit(solution)/shard_map/pack/pallas_call | solution.py:163
  10.0 9.6 %all-to-all-start.1 = ((bf16[16,4,64,256]{3,2,1,0:T(8,128)(2,1)}), bf16[16,4,64,256]{3,2,1,0:T(8,128)(2,1)S(1)}, u32[]{:S(2)}, u32[]{:S(2)}) async-start(bf16[16,4,64,256]{3,2,1,0:T(8,128)(2,1)} %pack.3), calls=%async_computation.1 | async-start | bytes 4194304 | tf_op jit(solution)/shard_map/all_to_all | solution.py:274
  19.6 9.3 %pack.2 = bf16[16,3,64,256]{3,2,1,0:T(8,128)(2,1)} custom-call(bf16[3,64,4096]{2,1,0:T(8,128)(2,1)} %bitcast.29), custom_call_target="tpu_custom_call" | custom-call | tf_op jit(solution)/shard_map/pack/pallas_call | solution.py:163
  28.9 0.0 copy-start.3
  28.9 41.3 %all-to-all-done.1.raw_ref = bf16[16,4,64,256]{3,2,1,0:T(8,128)(2,1)S(1)} async-done(((bf16[16,4,64,256]{3,2,1,0:T(8,128)(2,1)}), bf16[16,4,64,256]{3,2,1,0:T(8,128)(2,1)S(1)}, u32[]{:S(2)}, u32[]{:S(2)}) %all-to-all-start.1) | async-done | bytes 2097184 | tf_op jit(solution)/shard_map/all_to_all | solution.py:274
  70.2 0.0 copy-start
  70.2 1.3 copy-done
  71.5 3.7 %all-to-all-start = ((bf16[16,3,64,256]{3,2,1,0:T(8,128)(2,1)}), bf16[16,3,64,256]{3,2,1,0:T(8,128)(2,1)S(1)}, u32[]{:S(2)}, u32[]{:S(2)}) async-start(bf16[16,3,64,256]{3,2,1,0:T(8,128)(2,1)} %pack.2), calls=%async_computation | async-start | bytes 3145728 | tf_op jit(solution)/shard_map/all_to_all | solution.py:274
  75.2 0.7 constant_dynamic-slice_fusion
  76.0 0.0 copy-done.3
  76.0 0.0 copy-start.1
  76.0 1.6 copy-done.1
  77.6 0.0 copy-start.2
  77.6 10.4 %backward.1 = (bf16[16,4,64,256]{3,2,1,0:T(8,128)(2,1)}, f32[2,2,1,128]{3,2,1,0:T(1,128)S(1)}) custom-call(bf16[16,4,64,256]{3,2,1,0:T(8,128)(2,1)S(1)} %copy-done.1, f32[2,2,1,128]{3,2,1,0:T(1,128)S(1)} %bitcast.27, s32[8,128]{1,0:T(8,128)S(1)} %bitcast.28), custom_call_target="tpu_custom_call" | custom-call | flops 1610612736 | bytes 3670016 | tf_op jit(solution)/shard_map/backward/pallas_call | solution.py:206
  87.9 26.8 %all-to-all-done.raw_ref = bf16[16,3,64,256]{3,2,1,0:T(8,128)(2,1)S(1)} async-done(((bf16[16,3,64,256]{3,2,1,0:T(8,128)(2,1)}), bf16[16,3,64,256]{3,2,1,0:T(8,128)(2,1)S(1)}, u32[]{:S(2)}, u32[]{:S(2)}) %all-to-all-start) | async-done | bytes 1572896 | tf_op jit(solution)/shard_map/all_to_all | solution.py:274
  114.7 0.0 copy-done.2
  114.7 4.8 %forward.1 = bf16[16,4,64,256]{3,2,1,0:T(8,128)(2,1)} custom-call(bf16[16,3,64,256]{3,2,1,0:T(8,128)(2,1)S(1)} %all-to-all-done.raw_ref, f32[2,2,1,128]{3,2,1,0:T(1,128)S(1)} %bitcast.24, s32[8,128]{1,0:T(8,128)S(1)} %bitcast.25, bf16[16,4,64,256]{3,2,1,0:T(8,128)(2,1)} %get-tuple-element.7._), custom_call_target="tpu_custom_call", output_to_operand_aliasing={{}: (3, {})} | custom-call | flops 536870912 | bytes 2097152 | tf_op jit(solution)/shard_map/forward/pallas_call | solution.py:246
  119.5 0.0 copy-start.4
  119.5 4.6 %all-to-all-start.2 = ((bf16[16,4,64,256]{3,2,1,0:T(8,128)(2,1)}), bf16[16,4,64,256]{3,2,1,0:T(8,128)(2,1)}, u32[]{:S(2)}, u32[]{:S(2)}) async-start(bf16[16,4,64,256]{3,2,1,0:T(8,128)(2,1)} %forward.1), calls=%async_computation.2 | async-start | bytes 4194304 | tf_op jit(solution)/shard_map/all_to_all | solution.py:274
  124.1 0.0 copy-done.4
  124.1 1.1 collective-permute-start
  125.2 3.6 %collective-permute-done = f32[2,2,128]{2,1,0:T(2,128)S(1)} collective-permute-done((f32[2,2,128]{2,1,0:T(2,128)S(1)}, f32[2,2,128]{2,1,0:T(2,128)S(1)}, u32[]{:S(2)}, u32[]{:S(2)}) %collective-permute-start) | collective-permute-done | bytes 2080 | tf_op jit(solution)/shard_map/ppermute | solution.py:310
  128.7 9.2 %psum.7 = f32[1,2,2,128]{3,2,1,0:T(2,128)} all-reduce(f32[1,2,2,128]{3,2,1,0:T(2,128)S(1)} %fusion), channel_id=1, replica_groups=mesh['pipe'=4,'head'=16,'dp'=4] {'dp'}, use_global_device_ids=true, to_apply=%region_0.0 | all-reduce | flops 512 | bytes 4096 | tf_op jit(solution)/shard_map/psum | solution.py:311
  137.9 35.6 %all-to-all-done.2.in_ref = bf16[16,4,64,256]{3,2,1,0:T(8,128)(2,1)} async-done(((bf16[16,4,64,256]{3,2,1,0:T(8,128)(2,1)}), bf16[16,4,64,256]{3,2,1,0:T(8,128)(2,1)}, u32[]{:S(2)}, u32[]{:S(2)}) %all-to-all-start.2) | async-done | bytes 2097184 | tf_op jit(solution)/shard_map/all_to_all | solution.py:274
  173.5 9.4 %unpack.1 = (bf16[3,64,4096]{2,1,0:T(8,128)(2,1)}, bf16[64,4096]{1,0:T(8,128)(2,1)}) custom-call(bf16[16,4,64,256]{3,2,1,0:T(8,128)(2,1)} %all-to-all-done.2.in_ref), custom_call_target="tpu_custom_call" | custom-call | tf_op jit(solution)/shard_map/unpack/pallas_call | solution.py:182
  (2 shorter events, 0.0 us)
Async XLA Ops:
  10.0 60.1 %all-to-all-start.1 = ((bf16[16,4,64,256]{3,2,1,0:T(8,128)(2,1)}), bf16[16,4,64,256]{3,2,1,0:T(8,128)(2,1)S(1)}, u32[]{:S(2)}, u32[]{:S(2)}) async-start(bf16[16,4,64,256]{3,2,1,0:T(8,128)(2,1)} %pack.3), calls=%async_computation.1 | async-start | bytes 4194304 | tf_op jit(solution)/shard_map/all_to_all | solution.py:274
  28.9 47.1 %copy-start.3 = (s32[1,1,1024]{2,1,0:T(1,128)S(1)}, s32[1,1,1024]{2,1,0:T(1,128)}, u32[]{:S(2)}) copy-start(s32[1,1,1024]{2,1,0:T(1,128)} %param.11) | copy-start | bytes 12292
  70.2 1.3 copy-start
  71.5 43.2 %all-to-all-start = ((bf16[16,3,64,256]{3,2,1,0:T(8,128)(2,1)}), bf16[16,3,64,256]{3,2,1,0:T(8,128)(2,1)S(1)}, u32[]{:S(2)}, u32[]{:S(2)}) async-start(bf16[16,3,64,256]{3,2,1,0:T(8,128)(2,1)} %pack.2), calls=%async_computation | async-start | bytes 3145728 | tf_op jit(solution)/shard_map/all_to_all | solution.py:274
  76.0 1.6 copy-start.1
  77.6 37.1 %copy-start.2 = (s32[1,1,1024]{2,1,0:T(1,128)S(1)}, s32[1,1,1024]{2,1,0:T(1,128)}, u32[]{:S(2)}) copy-start(s32[1,1,1024]{2,1,0:T(1,128)} %param.10) | copy-start | bytes 12292
  119.5 4.6 %copy-start.4 = (f32[1,1,2,2,2,128]{5,4,3,2,1,0:T(2,128)S(1)}, f32[1,1,2,2,2,128]{5,4,3,2,1,0:T(2,128)}, u32[]{:S(2)}) copy-start(f32[1,1,2,2,2,128]{5,4,3,2,1,0:T(2,128)} %param.13) | copy-start | bytes 12292
  119.5 54.0 %all-to-all-start.2 = ((bf16[16,4,64,256]{3,2,1,0:T(8,128)(2,1)}), bf16[16,4,64,256]{3,2,1,0:T(8,128)(2,1)}, u32[]{:S(2)}, u32[]{:S(2)}) async-start(bf16[16,4,64,256]{3,2,1,0:T(8,128)(2,1)} %forward.1), calls=%async_computation.2 | async-start | bytes 4194304 | tf_op jit(solution)/shard_map/all_to_all | solution.py:274
  124.1 4.6 %collective-permute-start = (f32[2,2,128]{2,1,0:T(2,128)S(1)}, f32[2,2,128]{2,1,0:T(2,128)S(1)}, u32[]{:S(2)}, u32[]{:S(2)}) collective-permute-start(f32[2,2,128]{2,1,0:T(2,128)S(1)} %bitcast_add_fusion), channel_id=1, source_target_pairs={{0,192},{64,128},{128,64},{192,0},{1,193},{65,129},{129,65},{193,1... | collective-permute-start | bytes 6152 | tf_op jit(solution)/shard_map/ppermute | solution.py:310

commit v2 on v1

v2 whole, which is shorter than its diff:
```python
import functools
import math

import jax
import jax.numpy as jnp
from jax import lax
from jax.experimental import pallas as pl
from jax.experimental.pallas import tpu as pltpu
from jax.sharding import PartitionSpec as P

EPS = 1e-06
LONGEST = 512
BLOCK = 128
NT = (((1,), (1,)), ((), ()))
NN = (((1,), (0,)), ((), ()))
F32 = jnp.float32
BF16 = jnp.bfloat16


def dot(left, right, dims=NN):
    return lax.dot_general(left, right, dims, preferred_element_type=F32)


def unit_of(raw):
    values = raw.astype(F32)
    recip = lax.rsqrt(jnp.mean(values * values, axis=-1, keepdims=True) + EPS)
    return values * recip, recip


def starts_of(docs):
    first = jnp.zeros(docs.shape, jnp.int32)
    for value in range(3):
        count = jnp.sum((docs == value).astype(jnp.int32))
        first = first + jnp.where(docs > value, count, 0)
    return first


def window(block):
    low = max(0, block * BLOCK - LONGEST)
    return low, (block + 1) * BLOCK


def probs_of(keys, query, start, low, high):
    scores = dot(keys, query, NT)
    factor = math.log2(math.e) / math.sqrt(query.shape[-1])
    rows = lax.broadcasted_iota(jnp.int32, (BLOCK, BLOCK), 0)
    cols = lax.broadcasted_iota(jnp.int32, (BLOCK, BLOCK), 1)
    pieces = []
    for at in range(low, high, BLOCK):
        piece = scores[at - low : at - low + BLOCK]
        allowed = rows >= start - at
        if at + BLOCK == high:
            allowed = allowed & (rows <= cols)
        pieces.append(jnp.where(allowed, piece, -1e30))
    peak = jnp.max(functools.reduce(jnp.maximum, pieces), axis=0, keepdims=True)
    pieces = [jnp.exp2((piece - peak) * factor) for piece in pieces]
    total = jnp.sum(functools.reduce(jnp.add, pieces), axis=0, keepdims=True)
    share = 1.0 / total
    return [piece * share for piece in pieces]


def flat(ref, kind):
    ranks, _, rows, dim = ref.shape
    return ref[:, kind].reshape(ranks * rows, dim)


def load_pieces(pieces, group_ref, raw_refs, sems):
    kinds = raw_refs.shape[2]
    loads = [
        pltpu.make_async_copy(group_ref.at[:, first : first + kinds], raw_refs.at[slot], sems.at[slot])
        for slot, (_, first) in enumerate(pieces)
    ]
    for load in loads:
        load.start()
    return loads


def store_kinds(result_ref, out_ref, first, count, sem):
    store = pltpu.make_async_copy(
        result_ref.at[:, first : first + count], out_ref.at[:, first : first + count], sem
    )
    store.start()
    return store


def forward_kernel(
    pieces, group_ref, gain_ref, doc_ref, out_ref,
    raw_refs, result_ref, load_sems, store_sems, query_ref, key_ref, value_t_ref,
):
    loads = load_pieces(pieces, group_ref, raw_refs, load_sems)
    stores = []
    rows, dim = group_ref.shape[2:]
    starts = starts_of(doc_ref[...])
    per = BLOCK // rows
    for slot, (head, _) in enumerate(pieces):
        loads[slot].wait()
        raw_ref = raw_refs.at[slot]
        gain = gain_ref[:, head]
        query_ref[slot] = (unit_of(flat(raw_ref, 0))[0] * gain[0]).astype(BF16)
        key_ref[slot] = (unit_of(flat(raw_ref, 1))[0] * gain[1]).astype(BF16)
        value_t_ref[slot] = flat(raw_ref, 2).T
        for block in range(query_ref.shape[1] // BLOCK):
            low, high = window(block)
            query = query_ref[slot, block * BLOCK : high]
            probs = probs_of(key_ref[slot, low:high], query, starts[block : block + 1], low, high)
            probs = jnp.concatenate([piece.astype(BF16) for piece in probs], axis=0)
            result = dot(value_t_ref[slot, :, low:high], probs).T.astype(BF16)
            result_ref[block * per : (block + 1) * per, slot] = result.reshape(per, rows, dim)
        stores.append(store_kinds(result_ref, out_ref, slot, 1, store_sems.at[slot, 0]))
    for store in stores:
        store.wait()


def norm_back(raw, grad, gain):
    unit, recip = unit_of(raw)
    normed = grad.astype(F32)
    scaled = normed * gain
    grad_in = recip * (scaled - unit * jnp.mean(scaled * unit, axis=-1, keepdims=True))
    return grad_in.astype(BF16), jnp.sum(normed * unit, axis=0, keepdims=True)


def backward_kernel(
    pieces, group_ref, gain_ref, doc_ref, out_ref, new_ref,
    raw_refs, result_ref, load_sems, store_sems, query_refs, key_refs, key_t_refs, value_t_refs, up_t_refs, probs_refs, dscore_refs,
):
    loads = load_pieces(pieces, group_ref, raw_refs, load_sems)
    stores = []
    rows, dim = group_ref.shape[2:]
    tokens = query_refs.shape[1]
    scale = 1.0 / math.sqrt(dim)
    starts = starts_of(doc_ref[...])
    per = BLOCK // rows
    blocks = tokens // BLOCK

    for slot, (head, _) in enumerate(pieces):
        loads[slot].wait()
        query_ref, key_ref, key_t_ref, value_t_ref, up_t_ref, probs_ref, dscore_ref = [
            refs.at[slot]
            for refs in (
                query_refs, key_refs, key_t_refs, value_t_refs, up_t_refs, probs_refs, dscore_refs
            )
        ]
        gain = gain_ref[:, head]
        kind_out = 3 * slot

        def part(kind, low, high, raw_ref=raw_refs.at[slot]):
            piece = raw_ref[low // rows : high // rows, kind]
            return piece.reshape(high - low, dim)

        query_ref[...] = (unit_of(part(0, 0, tokens))[0] * gain[0]).astype(BF16)
        key = (unit_of(part(1, 0, tokens))[0] * gain[1]).astype(BF16)
        key_ref[...] = key
        key_t_ref[...] = key.T
        value_t_ref[...] = part(2, 0, tokens).T
        up_t_ref[...] = part(3, 0, tokens).T
        new_query = jnp.zeros((1, dim), F32)
        new_key = jnp.zeros((1, dim), F32)
        for block in range(blocks):
            low, high = window(block)
            here = slice(block * BLOCK, high)
            span = slice(block * per, (block + 1) * per)
            query = query_ref[here]
            probs = probs_of(key_ref[low:high], query, starts[block : block + 1], low, high)
            rounded = jnp.concatenate([piece.astype(BF16) for piece in probs], axis=0)
            probs_ref[low:high, here] = rounded
            result_t = dot(value_t_ref[:, low:high], rounded)
            dsum = jnp.sum(up_t_ref[:, here].astype(F32) * result_t, axis=0, keepdims=True)
            dprob = dot(part(2, low, high), part(3, block * BLOCK, high), NT)
            dscore = jnp.concatenate(
                [
                    (piece * (dprob[at * BLOCK : (at + 1) * BLOCK] - dsum)).astype(BF16)
                    for at, piece in enumerate(probs)
                ],
                axis=0,
            )
            dscore_ref[low:high, here] = dscore
            grad = (dot(key_t_ref[:, low:high], dscore) * scale).T.astype(BF16)
            grad_in, new = norm_back(part(0, block * BLOCK, high), grad, gain[0])
            new_query = new_query + new
            result_ref[span, kind_out] = grad_in.reshape(per, rows, dim)
        stores.append(store_kinds(result_ref, out_ref, kind_out, 1, store_sems.at[slot, 0]))

        for block in range(blocks):
            low = block * BLOCK
            high = min(tokens, low + BLOCK + LONGEST)
            here = slice(low, low + BLOCK)
            span = slice(block * per, (block + 1) * per)
            grad = (dot(dscore_ref[here, low:high], query_ref[low:high]) * scale).astype(BF16)
            grad_in, new = norm_back(part(1, low, low + BLOCK), grad, gain[1])
            new_key = new_key + new
            result_ref[span, kind_out + 1] = grad_in.reshape(per, rows, dim)
            value_grad = dot(probs_ref[here, low:high], part(3, low, high)).astype(BF16)
            result_ref[span, kind_out + 2] = value_grad.reshape(per, rows, dim)
        stores.append(store_kinds(result_ref, out_ref, kind_out + 1, 2, store_sems.at[slot, 1]))
        new_ref[0, head] = new_query
        new_ref[1, head] = new_key
    for store in stores:
        store.wait()


ANYWHERE = pl.BlockSpec(memory_space=pl.ANY)
IN_VMEM = pl.BlockSpec(memory_space=pltpu.VMEM)
VMEM_LIMIT = 40 * 1024 * 1024
KINDS_IN = {"f": 3, "b": 4}
KINDS_OUT = {"f": 1, "b": 3}


def places(pieces, kinds):
    found, at = {}, 0
    for piece in pieces:
        found[piece] = at
        at += kinds[piece[0]]
    return found, at


def wait_all(copies):
    for copy in copies:
        copy.start()
    for copy in copies:
        copy.wait()


def pack_kernel(pieces, ranks, *refs):
    *in_refs, out_ref, held_ref, load_sems, store_sems = refs
    dim = out_ref.shape[-1]
    heads = held_ref.shape[2] // (ranks * dim)
    loads, at = [], 0
    for index, ref in enumerate(in_refs):
        kinds = ref.shape[0]
        loads.append(pltpu.make_async_copy(ref, held_ref.at[at : at + kinds], load_sems.at[index]))
        loads[-1].start()
        at += kinds
    spans, at, index = {}, 0, 0
    stores, slot = [], 0
    for number, (name, head) in enumerate(pieces):
        if name not in spans:
            spans[name] = at
            for _ in range(1 if name == "f" else 2):
                loads[index].wait()
                index += 1
            at += KINDS_IN[name]
        kinds = KINDS_IN[name]
        for rank in range(ranks):
            low = (rank * heads + head) * dim
            store = pltpu.make_async_copy(
                held_ref.at[spans[name] : spans[name] + kinds, :, low : low + dim],
                out_ref.at[rank, slot : slot + kinds],
                store_sems.at[number, rank],
            )
            store.start()
            stores.append(store)
        slot += kinds
    for store in stores:
        store.wait()


def pack(sources, pieces, ranks, dim):
    names = list(dict.fromkeys(name for name, _ in pieces))
    arrays = [array for name in names for array in sources[name]]
    rows, width = arrays[0].shape[1:]
    held = sum(array.shape[0] for array in arrays)
    kinds = places(pieces, KINDS_IN)[1]
    return pl.pallas_call(
        functools.partial(pack_kernel, pieces, ranks),
        in_specs=[ANYWHERE] * len(arrays),
        out_specs=ANYWHERE,
        out_shape=pltpu.HBM((ranks, kinds, rows, dim), arrays[0].dtype),
        scratch_shapes=[
            pltpu.VMEM((held, rows, width), arrays[0].dtype),
            pltpu.SemaphoreType.DMA((len(arrays),)),
            pltpu.SemaphoreType.DMA((len(pieces), ranks)),
        ],
        compiler_params=pltpu.CompilerParams(vmem_limit_bytes=VMEM_LIMIT),
        name="pack",
    )(*[pltpu.with_memory_space_constraint(array, pltpu.HBM) for array in arrays])


def unpack_kernel(count, in_ref, out_ref, sems):
    ranks, _, _, dim = in_ref.shape
    kinds = out_ref.shape[0]
    copies = []
    for head in range(count):
        for rank in range(ranks):
            low = (rank * count + head) * dim
            copies.append(
                pltpu.make_async_copy(
                    in_ref.at[rank, head * kinds : (head + 1) * kinds],
                    out_ref.at[:, :, low : low + dim],
                    sems.at[head, rank],
                )
            )
    wait_all(copies)


def unpack(array, heads):
    ranks, kinds, rows, dim = array.shape
    return pl.pallas_call(
        functools.partial(unpack_kernel, heads),
        in_specs=[ANYWHERE],
        out_specs=ANYWHERE,
        out_shape=pltpu.HBM((kinds // heads, rows, ranks * heads * dim), array.dtype),
        scratch_shapes=[pltpu.SemaphoreType.DMA((heads, ranks))],
        compiler_params=pltpu.CompilerParams(vmem_limit_bytes=VMEM_LIMIT),
        name="unpack",
    )(array)


def attend(name, group, pieces, gain, docs):
    ranks, _, rows, dim = group.shape
    tokens = ranks * rows
    count = len(pieces)
    row_major = pltpu.VMEM((count, tokens, dim), BF16)
    col_major = pltpu.VMEM((count, dim, tokens), BF16)
    square = pltpu.VMEM((count, tokens, tokens), BF16)
    kinds_in, kinds_out = KINDS_IN[name], KINDS_OUT[name] * count
    scratch = [
        pltpu.VMEM((count, ranks, kinds_in, rows, dim), BF16),
        pltpu.VMEM((ranks, kinds_out, rows, dim), BF16),
        pltpu.SemaphoreType.DMA((count,)),
        pltpu.SemaphoreType.DMA((count, 2)),
        row_major,
        row_major,
        col_major,
    ]
    out_shape = [pltpu.HBM((ranks, kinds_out, rows, dim), group.dtype)]
    if name == "b":
        scratch += [col_major, col_major, square, square]
        out_shape.append(jax.ShapeDtypeStruct(gain.shape, F32))
    dots = 2 if name == "f" else 6
    return pl.pallas_call(
        functools.partial(forward_kernel if name == "f" else backward_kernel, pieces),
        in_specs=[ANYWHERE, IN_VMEM, IN_VMEM],
        out_specs=[ANYWHERE, IN_VMEM][: len(out_shape)],
        out_shape=out_shape,
        scratch_shapes=scratch,
        compiler_params=pltpu.CompilerParams(vmem_limit_bytes=VMEM_LIMIT),
        cost_estimate=pl.CostEstimate(
            flops=count * dots * tokens * tokens * dim,
            bytes_accessed=count * tokens * dim * 2 * (KINDS_IN[name] + KINDS_OUT[name]),
            transcendentals=count * tokens * tokens // 2,
        ),
        name="forward" if name == "f" else "backward",
    )(pltpu.with_memory_space_constraint(group, pltpu.HBM), gain, docs)


def exchange(value):
    return lax.all_to_all(value, "head", split_axis=0, concat_axis=0, tiled=True)


def after(value, earlier):
    return value if earlier is None else lax.optimization_barrier((value, earlier))[0]


F0, F1, B0, B1 = ("f", 0), ("f", 1), ("b", 0), ("b", 1)
PLANS = (
    (((B0, B1, F0, F1),), ("f", "b")),
    (((B0, B1), (F0, F1)), ("b", "f")),
)
TAIL = False


def branch(plan, fwd_raw, bwd_raw, upstream, gain_down, gain_up, fwd_docs, bwd_docs, accum):
    ranks = lax.axis_size("head")
    dim = gain_down.shape[-1]
    sources = {"f": [fwd_raw], "b": [bwd_raw, upstream]}
    gains = {"f": gain_down, "b": gain_up}
    docs = {"f": fwd_docs, "b": bwd_docs}
    ins, outs = plan
    latest, where = None, {}
    for pieces in ins:
        latest = exchange(after(pack(sources, pieces, ranks, dim), latest))
        for (name, head), first in places(pieces, KINDS_IN)[0].items():
            where.setdefault(name, (latest, []))[1].append((head, first))
    held, earlier = {}, None
    for index, name in enumerate(outs):
        group, pieces = where[name]
        results, *new = attend(name, after(group, earlier), tuple(pieces), gains[name], docs[name])
        if new:
            total = accum + jnp.stack([jnp.zeros_like(accum[0]), new[0].reshape(accum[0].shape)])
        earlier = results
        held[name] = after(results, latest)
        if not TAIL or index + 1 < len(outs):
            latest = exchange(held[name])
            held[name] = unpack(latest, 2)
    sums = lax.psum(total, "dp")
    return held["b"], held["f"], lax.optimization_barrier(sums)


def body(fwd_qkv, bwd_qkv, bwd_grad_out, fwd_doc, bwd_doc, norm_gain, grad_acc):
    ranks = lax.axis_size("head")
    pipe_count = lax.axis_size("pipe")
    pipe_at = lax.axis_index("pipe")
    head_at = lax.axis_index("head")
    tokens = fwd_qkv.shape[2]
    width = fwd_qkv.shape[4]
    dim = norm_gain.shape[3]
    local_heads = norm_gain.shape[2] // ranks

    def gain_of(section):
        part = lax.dynamic_slice(
            norm_gain, (section, 0, head_at * local_heads, 0), (1, 2, local_heads, dim)
        )
        return part.reshape(2, local_heads, 1, dim)

    args = (
        fwd_qkv.reshape(tokens, 3, width).transpose(1, 0, 2),
        bwd_qkv.reshape(tokens, 3, width).transpose(1, 0, 2),
        bwd_grad_out.reshape(1, tokens, width),
        gain_of(pipe_at),
        gain_of(pipe_count - 1 - pipe_at),
        fwd_doc.reshape(-1, BLOCK),
        bwd_doc.reshape(-1, BLOCK),
        grad_acc.reshape(2, 2, local_heads, dim),
    )
    qkv_grad, fwd_out, sums = lax.cond(
        pipe_at % 2 == 0,
        functools.partial(branch, PLANS[0]),
        functools.partial(branch, PLANS[1]),
        *args,
    )
    if TAIL:
        if PLANS[0][1][-1] == "f":
            fwd_out = unpack(exchange(fwd_out), local_heads)
        else:
            qkv_grad = unpack(exchange(qkv_grad), local_heads)
    mirrored = lax.ppermute(sums[1], "pipe", [(at, pipe_count - 1 - at) for at in range(pipe_count)])
    return (
        fwd_out.reshape(1, 1, tokens, width),
        qkv_grad.transpose(1, 0, 2).reshape(1, 1, tokens, 3, width),
        (sums[0] + mirrored).reshape(1, 2, local_heads, dim),
    )


def solution(mesh):
    in_specs = (
        P("dp", "pipe", "head", None, None),
        P("dp", "pipe", "head", None, None),
        P("dp", "pipe", "head", None),
        P("dp", "pipe", None),
        P("dp", "pipe", None),
        P(),
        P("dp", "pipe", None, None, "head", None),
    )
    out_specs = (
        P("dp", "pipe", "head", None),
        P("dp", "pipe", "head", None, None),
        P("pipe", None, "head", None),
    )
    return jax.shard_map(body, mesh=mesh, in_specs=in_specs, out_specs=out_specs, check_vma=False)
```

time: 184 us -> 159 us (0.86)
  waiting for transfers between devices: 107 us -> 20.9 us
  blocking collectives: 9.16 us -> 91.3 us
  Pallas kernels: 43.3 us -> 22.9 us
  local copies, waits for them, and re-layouts: 3.66 us -> 0.74 us
    all_to_all x3 -> x2, waiting for transfers between devices: 104 us -> 19.6 us  [exchange(): lax.all_to_all(value, 'head', split_axis=0, concat_axis=0, tiled=True)]
    all_to_all x0 -> x1, blocking collectives: none -> 82.7 us  [exchange(): lax.all_to_all(value, 'head', split_axis=0, concat_axis=0, tiled=True)]
    pallas_call x5, Pallas kernels: 43.3 us -> 22.9 us  [the longest x2 16.5 us: attend(): pl.pallas_call(functools.partial(forward_kernel if name == 'f' else backw...]
    ppermute x1, starting transfers between devices: 1.06 us -> 7.66 us  [body(): lax.ppermute(sums[1], 'pipe', [(at, pipe_count - 1 - at) for at in range(...]
    all_to_all x3 -> x2, starting transfers between devices: 17.9 us -> 11.8 us  [exchange(): lax.all_to_all(value, 'head', split_axis=0, concat_axis=0, tiled=True)]
    unnamed x10 -> x0, local copies, waits for them, and re-layouts: 2.93 us -> none
    ppermute x1, waiting for transfers between devices: 3.56 us -> 1.31 us  [body(): lax.ppermute(sums[1], 'pipe', [(at, pipe_count - 1 - at) for at in range(...]
  transfers between devices with their start and end apart: 4 -> 3, of which waited for: 4 -> 3; matrix products, arithmetic and copies ran while one was open for 0% -> 0% of each run, Pallas kernels for 11% -> 8%
where the time goes in v2:
time: 159 us; the launch traced here: 157 us
  blocking collectives  91.3 us (57%)
  Pallas kernels  22.9 us (14%)
  waiting for transfers between devices  20.9 us (13%)
  starting transfers between devices  19.4 us (12%)
    all_to_all x1, blocking collectives, exchange(): lax.all_to_all(value, 'head', split_axis=0, concat_axis=0, tiled=True)  82.7 us
    all_to_all x2, waiting for transfers between devices, exchange(): lax.all_to_all(value, 'head', split_axis=0, concat_axis=0, tiled=True)  19.6 us
    pallas_call x2, Pallas kernels, attend(): pl.pallas_call(functools.partial(forward_kernel if name == 'f' else backw...  16.5 us
    all_to_all x2, starting transfers between devices, exchange(): lax.all_to_all(value, 'head', split_axis=0, concat_axis=0, tiled=True)  11.8 us
    psum x1, blocking collectives, branch(): sums = lax.psum(total, 'dp')  8.62 us
    ppermute x1, starting transfers between devices, body(): lax.ppermute(sums[1], 'pipe', [(at, pipe_count - 1 - at) for at in range(...  7.66 us
    pallas_call x1, Pallas kernels, pack(): pl.pallas_call(functools.partial(pack_kernel, pieces, ranks), in_specs=[A...  3.89 us
  transfers between devices with their start and end apart: 3, of which 3 were waited for; matrix products, arithmetic and copies ran while one was open for 0% of the time, Pallas kernels for 8%

profile of v2, /device:TPU:2, one launch (start us, length us, event | category | flops | bytes accessed | tf_op | source)
XLA Modules:
  0.0 156.6 jit_solution(45761520036900802)
XLA Ops:
  0.6 0.7 constant_dynamic-slice_fusion
  1.4 145.7 %conditional.1 = (bf16[3,64,4096]{2,1,0:T(8,128)(2,1)}, f32[2,2,2,128]{3,2,1,0:T(2,128)S(1)}, bf16[1,1,64,4096]{3,2,1,0:T(8,128)(2,1)}) conditional(s32[]{:T(128)} %convert_element_type.3, (bf16[3,64,4096]{2,1,0:T(8,128)(2,1)}, bf16[1,64,4096]{2,1,0:T(8,128)(2,1)}, f32[2,2,1,128]{3,2,1,0:T(1,128)S(1)}, s32[8,128]{1,0:T(8,128)}, ...), branch_computations={%region_0.2_spmd, %region_2.4_spmd} | conditional | flops 2147485696 | bytes 37816612 | solution.py:415
  1.4 3.9 %pack.5 = bf16[16,14,64,128]{3,2,1,0:T(8,128)(2,1)} custom-call(bf16[3,64,4096]{2,1,0:T(8,128)(2,1)} %get-tuple-element.47.refs_0_, bf16[1,64,4096]{2,1,0:T(8,128)(2,1)} %get-tuple-element.48.refs_1_, bf16[3,64,4096]{2,1,0:T(8,128)(2,1)} %get-tuple-element.49.refs_2_), custom_call_target="tpu_custom_call" | custom-call | tf_op jit(solution)/shard_map/cond/branch_1_fun/pack/pallas_call | solution.py:263
  5.3 0.0 copy-start.3
  5.3 82.7 %all_to_all.28.group_ref = bf16[16,14,64,128]{3,2,1,0:T(8,128)(2,1)} all-to-all(bf16[16,14,64,128]{3,2,1,0:T(8,128)(2,1)} %pack.5), channel_id=1, replica_groups=mesh['pipe'=4,'head'=16,'dp'=4] {'head'}, dimensions={0} | all-to-all | bytes 7340032 | tf_op jit(solution)/shard_map/cond/branch_1_fun/all_to_all | solution.py:347
  88.0 0.0 copy-done.3
  88.0 0.0 copy-start.7
  88.0 5.5 %forward.3 = bf16[16,2,64,128]{3,2,1,0:T(8,128)(2,1)} custom-call(bf16[16,14,64,128]{3,2,1,0:T(8,128)(2,1)} %all_to_all.28.group_ref, f32[2,2,1,128]{3,2,1,0:T(1,128)S(1)} %get-tuple-element.50.gain_ref, s32[8,128]{1,0:T(8,128)S(1)} %copy-done.3), custom_call_target="tpu_custom_call" | custom-call | flops 536870912 | bytes 2097152 | tf_op jit(solution)/shard_map/cond/branch_1_fun/forward/pallas_call | solution.py:330
  93.4 5.1 %all-to-all-start.5 = ((bf16[16,2,64,128]{3,2,1,0:T(8,128)(2,1)}), bf16[16,2,64,128]{3,2,1,0:T(8,128)(2,1)S(1)}, u32[]{:S(2)}, u32[]{:S(2)}) async-start(bf16[16,2,64,128]{3,2,1,0:T(8,128)(2,1)} %forward.3), calls=%async_computation.5 | async-start | bytes 1048576 | tf_op jit(solution)/shard_map/cond/branch_1_fun/all_to_all | solution.py:347
  98.5 0.0 copy-done.7
  98.5 11.1 %backward.3 = (bf16[16,6,64,128]{3,2,1,0:T(8,128)(2,1)}, f32[2,2,1,128]{3,2,1,0:T(1,128)S(1)}) custom-call(bf16[16,14,64,128]{3,2,1,0:T(8,128)(2,1)} %all_to_all.28.group_ref, f32[2,2,1,128]{3,2,1,0:T(1,128)S(1)} %get-tuple-element.53.gain_ref, s32[8,128]{1,0:T(8,128)S(1)} %copy-done.7), custom_call_target="tpu_custom_call" | custom-call | flops 1610612736 | bytes 3670016 | tf_op jit(solution)/shard_map/cond/branch_1_fun/backward/pallas_call | solution.py:330
  109.6 3.6 %all-to-all-done.5.in_ref = bf16[16,2,64,128]{3,2,1,0:T(8,128)(2,1)S(1)} async-done(((bf16[16,2,64,128]{3,2,1,0:T(8,128)(2,1)}), bf16[16,2,64,128]{3,2,1,0:T(8,128)(2,1)S(1)}, u32[]{:S(2)}, u32[]{:S(2)}) %all-to-all-start.5) | async-done | bytes 524320 | tf_op jit(solution)/shard_map/cond/branch_1_fun/all_to_all | solution.py:347
  113.2 0.0 copy-start.5
  113.2 6.7 %all-to-all-start.6 = ((bf16[16,6,64,128]{3,2,1,0:T(8,128)(2,1)}), bf16[16,6,64,128]{3,2,1,0:T(8,128)(2,1)S(1)}, u32[]{:S(2)}, u32[]{:S(2)}) async-start(bf16[16,6,64,128]{3,2,1,0:T(8,128)(2,1)} %get-tuple-element.57), calls=%async_computation.6 | async-start | bytes 3145728 | tf_op jit(solution)/shard_map/cond/branch_1_fun/all_to_all | solution.py:347
  119.9 0.0 copy-done.5
  119.9 8.6 %psum.13 = f32[2,2,2,128]{3,2,1,0:T(2,128)S(1)} all-reduce(f32[2,2,2,128]{3,2,1,0:T(2,128)S(1)} %pad_add_fusion.1), channel_id=1, replica_groups=mesh['pipe'=4,'head'=16,'dp'=4] {'dp'}, use_global_device_ids=true, to_apply=%region_3.3 | all-reduce | flops 1024 | bytes 8192 | tf_op jit(solution)/shard_map/cond/branch_1_fun/psum | solution.py:385
  128.5 1.1 unpack.7
  129.6 16.0 %all-to-all-done.6.in_ref = bf16[16,6,64,128]{3,2,1,0:T(8,128)(2,1)S(1)} async-done(((bf16[16,6,64,128]{3,2,1,0:T(8,128)(2,1)}), bf16[16,6,64,128]{3,2,1,0:T(8,128)(2,1)S(1)}, u32[]{:S(2)}, u32[]{:S(2)}) %all-to-all-start.6) | async-done | bytes 1572896 | tf_op jit(solution)/shard_map/cond/branch_1_fun/all_to_all | solution.py:347
  145.6 1.4 unpack.6
  147.1 7.7 %collective-permute-start = (f32[2,2,128]{2,1,0:T(2,128)S(1)}, f32[2,2,128]{2,1,0:T(2,128)S(1)}, u32[]{:S(2)}, u32[]{:S(2)}) collective-permute-start(f32[2,2,128]{2,1,0:T(2,128)S(1)} %slice_bitcast_fusion), channel_id=1, source_target_pairs={{0,192},{64,128},{128,64},{192,0},{1,193},{65,129},{129,65},{193,1... | collective-permute-start | bytes 6152 | tf_op jit(solution)/shard_map/ppermute | solution.py:426
  154.7 1.3 collective-permute-done
  156.0 0.6 fusion
  (2 shorter events, 0.0 us)
Async XLA Ops:
  5.3 82.7 %copy-start.3 = (s32[8,128]{1,0:T(8,128)S(1)}, s32[8,128]{1,0:T(8,128)}, u32[]{:S(2)}) copy-start(s32[8,128]{1,0:T(8,128)} %get-tuple-element.51.doc_ref) | copy-start | bytes 12292 | tf_op jit(solution)/shard_map/cond
  88.0 10.5 %copy-start.7 = (s32[8,128]{1,0:T(8,128)S(1)}, s32[8,128]{1,0:T(8,128)}, u32[]{:S(2)}) copy-start(s32[8,128]{1,0:T(8,128)} %get-tuple-element.54.doc_ref) | copy-start | bytes 12292 | tf_op jit(solution)/shard_map/cond
  93.4 19.7 %all-to-all-start.5 = ((bf16[16,2,64,128]{3,2,1,0:T(8,128)(2,1)}), bf16[16,2,64,128]{3,2,1,0:T(8,128)(2,1)S(1)}, u32[]{:S(2)}, u32[]{:S(2)}) async-start(bf16[16,2,64,128]{3,2,1,0:T(8,128)(2,1)} %forward.3), calls=%async_computation.5 | async-start | bytes 1048576 | tf_op jit(solution)/shard_map/cond/branch_1_fun/all_to_all | solution.py:347
  113.2 6.7 %copy-start.5 = (f32[2,2,2,128]{3,2,1,0:T(2,128)S(1)}, f32[2,2,2,128]{3,2,1,0:T(2,128)}, u32[]{:S(2)}) copy-start(f32[2,2,2,128]{3,2,1,0:T(2,128)} %get-tuple-element.58) | copy-start | bytes 12292 | tf_op jit(solution)/shard_map/cond
  113.2 32.5 %all-to-all-start.6 = ((bf16[16,6,64,128]{3,2,1,0:T(8,128)(2,1)}), bf16[16,6,64,128]{3,2,1,0:T(8,128)(2,1)S(1)}, u32[]{:S(2)}, u32[]{:S(2)}) async-start(bf16[16,6,64,128]{3,2,1,0:T(8,128)(2,1)} %get-tuple-element.57), calls=%async_computation.6 | async-start | bytes 3145728 | tf_op jit(solution)/shard_map/cond/branch_1_fun/all_to_all | solution.py:347
  147.1 9.0 %collective-permute-start = (f32[2,2,128]{2,1,0:T(2,128)S(1)}, f32[2,2,128]{2,1,0:T(2,128)S(1)}, u32[]{:S(2)}, u32[]{:S(2)}) collective-permute-start(f32[2,2,128]{2,1,0:T(2,128)S(1)} %slice_bitcast_fusion), channel_id=1, source_target_pairs={{0,192},{64,128},{128,64},{192,0},{1,193},{65,129},{129,65},{193,1... | collective-permute-start | bytes 6152 | tf_op jit(solution)/shard_map/ppermute | solution.py:426

commit v3 on v2

v3 whole, which is shorter than its diff:
```python
import functools
import math

import jax
import jax.numpy as jnp
from jax import lax
from jax.experimental import pallas as pl
from jax.experimental.pallas import tpu as pltpu
from jax.sharding import PartitionSpec as P

EPS = 1e-06
LONGEST = 512
BLOCK = 128
NT = (((1,), (1,)), ((), ()))
NN = (((1,), (0,)), ((), ()))
F32 = jnp.float32
BF16 = jnp.bfloat16


def dot(left, right, dims=NN):
    return lax.dot_general(left, right, dims, preferred_element_type=F32)


def unit_of(raw):
    values = raw.astype(F32)
    recip = lax.rsqrt(jnp.mean(values * values, axis=-1, keepdims=True) + EPS)
    return values * recip, recip


def starts_of(docs):
    first = jnp.zeros(docs.shape, jnp.int32)
    for value in range(3):
        count = jnp.sum((docs == value).astype(jnp.int32))
        first = first + jnp.where(docs > value, count, 0)
    return first


def window(block):
    low = max(0, block * BLOCK - LONGEST)
    return low, (block + 1) * BLOCK


FORWARD_GROUP, BACKWARD_GROUP, KEY_GROUP = 8, 4, 4


def groups_of(count, blocks, size):
    items = [(slot, block) for block in range(blocks) for slot in range(count)]
    return [items[at : at + size] for at in range(0, len(items), size)]


def probs_of(scores, starts, spans, dim):
    factor = math.log2(math.e) / math.sqrt(dim)
    rows = lax.broadcasted_iota(jnp.int32, (BLOCK, BLOCK), 0)
    cols = lax.broadcasted_iota(jnp.int32, (BLOCK, BLOCK), 1)
    lists = []
    for score, start, (low, high) in zip(scores, starts, spans):
        pieces = []
        for at in range(low, high, BLOCK):
            allowed = rows >= start - at
            if at + BLOCK == high:
                allowed = allowed & (rows <= cols)
            pieces.append(jnp.where(allowed, score[at - low : at - low + BLOCK], -1e30))
        lists.append(pieces)
    peaks = [
        jnp.max(functools.reduce(jnp.maximum, pieces), axis=0, keepdims=True) for pieces in lists
    ]
    lists = [
        [jnp.exp2((piece - peak) * factor) for piece in pieces] for pieces, peak in zip(lists, peaks)
    ]
    shares = [
        1.0 / jnp.sum(functools.reduce(jnp.add, pieces), axis=0, keepdims=True) for pieces in lists
    ]
    return [[piece * share for piece in pieces] for pieces, share in zip(lists, shares)]


def flat(ref, kind):
    ranks, _, rows, dim = ref.shape
    return ref[:, kind].reshape(ranks * rows, dim)


def load_pieces(pieces, group_ref, raw_refs, sems):
    kinds = raw_refs.shape[2]
    loads = [
        pltpu.make_async_copy(group_ref.at[:, first : first + kinds], raw_refs.at[slot], sems.at[slot])
        for slot, (_, first) in enumerate(pieces)
    ]
    for load in loads:
        load.start()
    return loads


def store_kinds(result_ref, out_ref, base, first, count, sem):
    out_part = out_ref.at[:, base + first : base + first + count]
    store = pltpu.make_async_copy(result_ref.at[:, first : first + count], out_part, sem)
    store.start()
    return store


def forward_kernel(pieces, base, group_ref, gain_ref, doc_ref, *refs):
    (
        out_ref, raw_refs, result_ref, load_sems, store_sems, query_ref, key_ref, value_t_ref,
    ) = refs[-8:]
    loads = load_pieces(pieces, group_ref, raw_refs, load_sems)
    rows, dim = group_ref.shape[2:]
    starts = starts_of(doc_ref[...])
    per = BLOCK // rows
    for slot, (head, _) in enumerate(pieces):
        loads[slot].wait()
        raw_ref = raw_refs.at[slot]
        gain = gain_ref[:, head]
        query_ref[slot] = (unit_of(flat(raw_ref, 0))[0] * gain[0]).astype(BF16)
        key_ref[slot] = (unit_of(flat(raw_ref, 1))[0] * gain[1]).astype(BF16)
        value_t_ref[slot] = flat(raw_ref, 2).T
    for items in groups_of(len(pieces), query_ref.shape[1] // BLOCK, FORWARD_GROUP):
        spans = [window(block) for _, block in items]
        scores = [
            dot(key_ref[slot, low:high], query_ref[slot, block * BLOCK : high], NT)
            for (slot, block), (low, high) in zip(items, spans)
        ]
        probs = probs_of(scores, [starts[block : block + 1] for _, block in items], spans, dim)
        probs = [jnp.concatenate([piece.astype(BF16) for piece in every], axis=0) for every in probs]
        results = [
            dot(value_t_ref[slot, :, low:high], prob)
            for (slot, _), (low, high), prob in zip(items, spans, probs)
        ]
        for (slot, block), result in zip(items, results):
            result = result.T.astype(BF16).reshape(per, rows, dim)
            result_ref[block * per : (block + 1) * per, slot] = result
    store_kinds(result_ref, out_ref, base, 0, len(pieces), store_sems.at[0, 0]).wait()


def norm_back(raw, grad, gain):
    unit, recip = unit_of(raw)
    normed = grad.astype(F32)
    scaled = normed * gain
    grad_in = recip * (scaled - unit * jnp.mean(scaled * unit, axis=-1, keepdims=True))
    return grad_in.astype(BF16), jnp.sum(normed * unit, axis=0, keepdims=True)


def backward_kernel(pieces, base, group_ref, gain_ref, doc_ref, *refs):
    (
        out_ref, new_ref, raw_refs, result_ref, load_sems, store_sems,
        query_refs, key_refs, key_t_refs, value_t_refs, up_t_refs, probs_refs, dscore_refs,
    ) = refs[-13:]
    loads = load_pieces(pieces, group_ref, raw_refs, load_sems)
    rows, dim = group_ref.shape[2:]
    tokens = query_refs.shape[1]
    scale = 1.0 / math.sqrt(dim)
    starts = starts_of(doc_ref[...])
    per = BLOCK // rows
    blocks = tokens // BLOCK
    count = len(pieces)

    def part(slot, kind, low, high):
        return raw_refs[slot, low // rows : high // rows, kind].reshape(high - low, dim)

    for slot, (head, _) in enumerate(pieces):
        loads[slot].wait()
        gain = gain_ref[:, head]
        query_refs[slot] = (unit_of(part(slot, 0, 0, tokens))[0] * gain[0]).astype(BF16)
        key = (unit_of(part(slot, 1, 0, tokens))[0] * gain[1]).astype(BF16)
        key_refs[slot] = key
        key_t_refs[slot] = key.T
        value_t_refs[slot] = part(slot, 2, 0, tokens).T
        up_t_refs[slot] = part(slot, 3, 0, tokens).T
    new_query = [jnp.zeros((1, dim), F32)] * count
    new_key = [jnp.zeros((1, dim), F32)] * count
    for items in groups_of(count, blocks, BACKWARD_GROUP):
        spans = [window(block) for _, block in items]
        heres = [slice(block * BLOCK, (block + 1) * BLOCK) for _, block in items]
        every = [(slot, low, high, here) for (slot, _), (low, high), here in zip(items, spans, heres)]
        scores = [
            dot(key_refs[slot, low:high], query_refs[slot, here], NT) for slot, low, high, here in every
        ]
        dprobs = [
            dot(part(slot, 2, low, high), part(slot, 3, here.start, here.stop), NT)
            for slot, low, high, here in every
        ]
        probs = probs_of(scores, [starts[block : block + 1] for _, block in items], spans, dim)
        rounded = [jnp.concatenate([piece.astype(BF16) for piece in some], axis=0) for some in probs]
        results = [
            dot(value_t_refs[slot, :, low:high], some)
            for (slot, low, high, _), some in zip(every, rounded)
        ]
        for (slot, low, high, here), some in zip(every, rounded):
            probs_refs[slot, low:high, here] = some
        dsums = [
            jnp.sum(up_t_refs[slot, :, here].astype(F32) * result, axis=0, keepdims=True)
            for (slot, _, _, here), result in zip(every, results)
        ]
        dscores = [
            jnp.concatenate(
                [
                    (piece * (dprob[at * BLOCK : (at + 1) * BLOCK] - dsum)).astype(BF16)
                    for at, piece in enumerate(some)
                ],
                axis=0,
            )
            for some, dprob, dsum in zip(probs, dprobs, dsums)
        ]
        grads = [
            dot(key_t_refs[slot, :, low:high], dscore) * scale
            for (slot, low, high, _), dscore in zip(every, dscores)
        ]
        for (slot, low, high, here), dscore in zip(every, dscores):
            dscore_refs[slot, low:high, here] = dscore
        grads = [grad.T.astype(BF16) for grad in grads]
        for (slot, block), here, grad in zip(items, heres, grads):
            gain = gain_ref[0, pieces[slot][0]]
            grad_in, new = norm_back(part(slot, 0, here.start, here.stop), grad, gain)
            new_query[slot] = new_query[slot] + new
            span = slice(block * per, (block + 1) * per)
            result_ref[span, 3 * slot] = grad_in.reshape(per, rows, dim)

    for items in groups_of(count, blocks, KEY_GROUP):
        every = [
            (slot, slice(block * BLOCK, (block + 1) * BLOCK), min(tokens, (block + 1) * BLOCK + LONGEST))
            for slot, block in items
        ]
        grads = [
            dot(dscore_refs[slot, here, here.start : high], query_refs[slot, here.start : high])
            for slot, here, high in every
        ]
        value_grads = [
            dot(probs_refs[slot, here, here.start : high], part(slot, 3, here.start, high))
            for slot, here, high in every
        ]
        for (slot, block), here, grad, value_grad in zip(
            items, [here for _, here, _ in every], grads, value_grads
        ):
            gain = gain_ref[1, pieces[slot][0]]
            grad = (grad * scale).astype(BF16)
            grad_in, new = norm_back(part(slot, 1, here.start, here.stop), grad, gain)
            new_key[slot] = new_key[slot] + new
            span = slice(block * per, (block + 1) * per)
            result_ref[span, 3 * slot + 1] = grad_in.reshape(per, rows, dim)
            result_ref[span, 3 * slot + 2] = value_grad.astype(BF16).reshape(per, rows, dim)
    store = store_kinds(result_ref, out_ref, base, 0, 3 * count, store_sems.at[0, 0])
    for slot, (head, _) in enumerate(pieces):
        new_ref[0, head] = new_query[slot]
        new_ref[1, head] = new_key[slot]
    store.wait()


ANYWHERE = pl.BlockSpec(memory_space=pl.ANY)
IN_VMEM = pl.BlockSpec(memory_space=pltpu.VMEM)
VMEM_LIMIT = 40 * 1024 * 1024
KINDS_IN = {"f": 3, "b": 4}
KINDS_OUT = {"f": 1, "b": 3}


def places(pieces, kinds):
    found, at = {}, 0
    for piece in pieces:
        found[piece] = at
        at += kinds[piece[0]]
    return found, at


def pack_kernel(pieces, ranks, *refs):
    *in_refs, out_ref, held_ref, load_sems, store_sems = refs
    dim = out_ref.shape[-1]
    heads = held_ref.shape[2] // (ranks * dim)
    loads, at = [], 0
    for index, ref in enumerate(in_refs):
        kinds = ref.shape[0]
        loads.append(pltpu.make_async_copy(ref, held_ref.at[at : at + kinds], load_sems.at[index]))
        loads[-1].start()
        at += kinds
    spans, at, index = {}, 0, 0
    stores, slot = [], 0
    for number, (name, head) in enumerate(pieces):
        if name not in spans:
            spans[name] = at
            for _ in range(1 if name == "f" else 2):
                loads[index].wait()
                index += 1
            at += KINDS_IN[name]
        kinds = KINDS_IN[name]
        for rank in range(ranks):
            low = (rank * heads + head) * dim
            store = pltpu.make_async_copy(
                held_ref.at[spans[name] : spans[name] + kinds, :, low : low + dim],
                out_ref.at[rank, slot : slot + kinds],
                store_sems.at[number, rank],
            )
            store.start()
            stores.append(store)
        slot += kinds
    for store in stores:
        store.wait()


def pack(sources, pieces, ranks, dim):
    names = list(dict.fromkeys(name for name, _ in pieces))
    arrays = [array for name in names for array in sources[name]]
    rows, width = arrays[0].shape[1:]
    held = sum(array.shape[0] for array in arrays)
    kinds = places(pieces, KINDS_IN)[1]
    return pl.pallas_call(
        functools.partial(pack_kernel, pieces, ranks),
        in_specs=[ANYWHERE] * len(arrays),
        out_specs=ANYWHERE,
        out_shape=pltpu.HBM((ranks, kinds, rows, dim), arrays[0].dtype),
        scratch_shapes=[
            pltpu.VMEM((held, rows, width), arrays[0].dtype),
            pltpu.SemaphoreType.DMA((len(arrays),)),
            pltpu.SemaphoreType.DMA((len(pieces), ranks)),
        ],
        compiler_params=pltpu.CompilerParams(vmem_limit_bytes=VMEM_LIMIT),
        name="pack",
    )(*[pltpu.with_memory_space_constraint(array, pltpu.HBM) for array in arrays])


def unpack_kernel(count, in_ref, *refs):
    *out_refs, sems = refs
    ranks, _, _, dim = in_ref.shape
    copies, first = [], 0
    for number, out_ref in enumerate(out_refs):
        kinds = out_ref.shape[0]
        for head in range(count):
            for rank in range(ranks):
                low = (rank * count + head) * dim
                copies.append(
                    pltpu.make_async_copy(
                        in_ref.at[rank, first : first + kinds],
                        out_ref.at[:, :, low : low + dim],
                        sems.at[number, head, rank],
                    )
                )
            first += kinds
    for copy in copies:
        copy.start()
    for copy in copies:
        copy.wait()


def unpack(array, names, heads):
    ranks, _, rows, dim = array.shape
    return pl.pallas_call(
        functools.partial(unpack_kernel, heads),
        in_specs=[ANYWHERE],
        out_specs=[ANYWHERE] * len(names),
        out_shape=[
            pltpu.HBM((KINDS_OUT[name], rows, ranks * heads * dim), array.dtype) for name in names
        ],
        scratch_shapes=[pltpu.SemaphoreType.DMA((len(names), heads, ranks))],
        compiler_params=pltpu.CompilerParams(vmem_limit_bytes=VMEM_LIMIT),
        name="unpack",
    )(array)


def attend(name, group, pieces, gain, docs, kinds, base, out, settled):
    if settled:
        group = pltpu.with_memory_space_constraint(group, pltpu.HBM)
    ranks, _, rows, dim = group.shape
    tokens = ranks * rows
    count = len(pieces)
    row_major = pltpu.VMEM((count, tokens, dim), BF16)
    col_major = pltpu.VMEM((count, dim, tokens), BF16)
    square = pltpu.VMEM((count, tokens, tokens), BF16)
    kinds_in, kinds_out = KINDS_IN[name], KINDS_OUT[name] * count
    scratch = [
        pltpu.VMEM((count, ranks, kinds_in, rows, dim), BF16),
        pltpu.VMEM((ranks, kinds_out, rows, dim), BF16),
        pltpu.SemaphoreType.DMA((count,)),
        pltpu.SemaphoreType.DMA((count, 2)),
        row_major,
        row_major,
        col_major,
    ]
    out_shape = [pltpu.HBM((ranks, kinds, rows, dim), group.dtype)]
    if name == "b":
        scratch += [col_major, col_major, square, square]
        out_shape.append(jax.ShapeDtypeStruct(gain.shape, F32))
    dots = 2 if name == "f" else 6
    return pl.pallas_call(
        functools.partial(forward_kernel if name == "f" else backward_kernel, pieces, base),
        in_specs=[ANYWHERE, IN_VMEM, IN_VMEM] + [ANYWHERE] * len(out),
        out_specs=[ANYWHERE, IN_VMEM][: len(out_shape)],
        out_shape=out_shape,
        scratch_shapes=scratch,
        input_output_aliases={3: 0} if out else {},
        compiler_params=pltpu.CompilerParams(vmem_limit_bytes=VMEM_LIMIT),
        cost_estimate=pl.CostEstimate(
            flops=count * dots * tokens * tokens * dim,
            bytes_accessed=count * tokens * dim * 2 * (KINDS_IN[name] + KINDS_OUT[name]),
            transcendentals=count * tokens * tokens // 2,
        ),
        name="forward" if name == "f" else "backward",
    )(group, gain, docs, *out)


def exchange(value):
    return lax.all_to_all(value, "head", split_axis=0, concat_axis=0, tiled=True)


def after(value, earlier):
    return value if earlier is None else lax.optimization_barrier((value, earlier))[0]


def copy_kernel(in_ref, out_ref, sem):
    copy = pltpu.make_async_copy(in_ref, out_ref, sem)
    copy.start()
    copy.wait()


def into_hbm(array):
    return pl.pallas_call(
        copy_kernel,
        in_specs=[IN_VMEM],
        out_specs=ANYWHERE,
        out_shape=pltpu.HBM(array.shape, array.dtype),
        scratch_shapes=[pltpu.SemaphoreType.DMA(())],
        name="settle",
    )(array)


F0, F1, B0, B1 = ("f", 0), ("f", 1), ("b", 0), ("b", 1)
PLANS = (
    (((B0, B1, F0, F1),), (("b",), ("f",))),
    (((B0, B1), (F0, F1)), (("b", "f"),)),
)


def branch(plan, mirror, fwd_raw, bwd_raw, upstream, norm_gain, fwd_docs, bwd_docs, accum):
    ranks = lax.axis_size("head")
    pipe_count = lax.axis_size("pipe")
    pipe_at = lax.axis_index("pipe")
    heads, dim = norm_gain.shape[2] // ranks, norm_gain.shape[3]
    head_at = lax.axis_index("head") * heads
    sources = {"f": [fwd_raw], "b": [bwd_raw, upstream]}
    sections = {"f": pipe_at, "b": pipe_count - 1 - pipe_at}
    gains = {
        name: lax.dynamic_slice(norm_gain, (at, 0, head_at, 0), (1, 2, heads, dim)).reshape(
            2, heads, 1, dim
        )
        for name, at in sections.items()
    }
    docs = {"f": fwd_docs, "b": bwd_docs}
    ins, outs = plan
    latest, where = None, {}
    for pieces in ins:
        latest = exchange(after(pack(sources, pieces, ranks, dim), latest))
        for (name, head), first in places(pieces, KINDS_IN)[0].items():
            where.setdefault(name, (latest, []))[1].append((head, first))
    held, earlier = {}, None
    for names in outs:
        out, base = (), 0
        kinds = sum(KINDS_OUT[name] for name in names) * heads
        for name in names:
            group, pieces = where[name]
            results, *new = attend(
                name, after(group, earlier), tuple(pieces), gains[name], docs[name], kinds, base, out,
                len(ins) == 1 or group is not latest,
            )
            if new:
                up_local = accum[1] + new[0].reshape(accum[1].shape)
                mirrored = lax.ppermute(up_local, "pipe", mirror)
                total = lax.psum(accum[0] + mirrored, "dp")
            out, earlier = (results,), results
            base += KINDS_OUT[name] * heads
        latest = exchange(after(results, (latest, total) if held.get("b") is not None else latest))
        held.update(zip(names, unpack(latest, names, heads)))
    return held["b"], held["f"], into_hbm(total)


def body(fwd_qkv, bwd_qkv, bwd_grad_out, fwd_doc, bwd_doc, norm_gain, grad_acc):
    ranks = lax.axis_size("head")
    pipe_count = lax.axis_size("pipe")
    pipe_at = lax.axis_index("pipe")
    tokens = fwd_qkv.shape[2]
    width = fwd_qkv.shape[4]
    dim = norm_gain.shape[3]
    local_heads = norm_gain.shape[2] // ranks

    args = (
        fwd_qkv.reshape(tokens, 3, width).transpose(1, 0, 2),
        bwd_qkv.reshape(tokens, 3, width).transpose(1, 0, 2),
        bwd_grad_out.reshape(1, tokens, width),
        norm_gain,
        fwd_doc.reshape(-1, BLOCK),
        bwd_doc.reshape(-1, BLOCK),
        grad_acc.reshape(2, 2, local_heads, dim),
    )
    plans = [(at ^ (at >> 1)) & 1 for at in range(pipe_count)]
    mirrors = [
        [(at, pipe_count - 1 - at) for at in range(pipe_count) if plans[at] == plan]
        for plan in range(2)
    ]
    qkv_grad, fwd_out, total = lax.cond(
        (pipe_at ^ (pipe_at >> 1)) & 1 == 0,
        functools.partial(branch, PLANS[0], mirrors[0]),
        functools.partial(branch, PLANS[1], mirrors[1]),
        *args,
    )
    return (
        fwd_out.reshape(1, 1, tokens, width),
        qkv_grad.transpose(1, 0, 2).reshape(1, 1, tokens, 3, width),
        total.reshape(1, 2, local_heads, dim),
    )


def solution(mesh):
    in_specs = (
        P("dp", "pipe", "head", None, None),
        P("dp", "pipe", "head", None, None),
        P("dp", "pipe", "head", None),
        P("dp", "pipe", None),
        P("dp", "pipe", None),
        P(),
        P("dp", "pipe", None, None, "head", None),
    )
    out_specs = (
        P("dp", "pipe", "head", None),
        P("dp", "pipe", "head", None, None),
        P("pipe", None, "head", None),
    )
    return jax.shard_map(body, mesh=mesh, in_specs=in_specs, out_specs=out_specs, check_vma=False)
```

time: 159 us -> 151 us (0.950); the launches traced: 157 us -> 151 us
  blocking collectives: 91.3 us -> 9.19 us
  waiting for transfers between devices: 20.9 us -> 95.1 us
  starting transfers between devices: 19.4 us -> 22.7 us
    all_to_all x1 -> x0, blocking collectives: 82.7 us -> none  [exchange(): lax.all_to_all(value, 'head', split_axis=0, concat_axis=0, tiled=True)]
    all_to_all x2 -> x3, waiting for transfers between devices: 19.6 us -> 95.1 us  [exchange(): lax.all_to_all(value, 'head', split_axis=0, concat_axis=0, tiled=True)]
    all_to_all x2 -> x3, starting transfers between devices: 11.8 us -> 19 us  [exchange(): lax.all_to_all(value, 'head', split_axis=0, concat_axis=0, tiled=True)]
    ppermute x1, starting transfers between devices: 7.66 us -> 3.7 us  [branch(): mirrored = lax.ppermute(up_local, 'pipe', mirror)]
    pallas_call x2, Pallas kernels: 16.5 us -> 14.1 us  [attend(): pl.pallas_call(functools.partial(forward_kernel if name == 'f' else backw...]
  transfers between devices with their start and end apart: 3 -> 4, of which waited for: 3 -> 3; matrix products, arithmetic and copies ran while one was open for 0% -> 0% of each run, Pallas kernels for 8% -> 5%
where the time goes in v3:
time: 151 us
  waiting for transfers between devices  95.1 us (63%)
  starting transfers between devices  22.7 us (15%)
  Pallas kernels  21.7 us (14%)
  blocking collectives  9.19 us (6%)
    all_to_all x3, waiting for transfers between devices, exchange(): lax.all_to_all(value, 'head', split_axis=0, concat_axis=0, tiled=True)  95.1 us
    all_to_all x3, starting transfers between devices, exchange(): lax.all_to_all(value, 'head', split_axis=0, concat_axis=0, tiled=True)  19 us
    pallas_call x2, Pallas kernels, attend(): pl.pallas_call(functools.partial(forward_kernel if name == 'f' else backw...  14.1 us
    psum x1, blocking collectives, branch(): total = lax.psum(accum[0] + mirrored, 'dp')  9.19 us
    pallas_call x1, Pallas kernels, pack(): pl.pallas_call(functools.partial(pack_kernel, pieces, ranks), in_specs=[A...  3.91 us
    ppermute x1, starting transfers between devices, branch(): mirrored = lax.ppermute(up_local, 'pipe', mirror)  3.7 us
  transfers between devices with their start and end apart: 4, of which 3 were waited for; matrix products, arithmetic and copies ran while one was open for 0% of the time, Pallas kernels for 5%

profile of v3, /device:TPU:2, one launch (start us, length us, event | category | flops | bytes accessed | tf_op | source)
XLA Modules:
  0.0 150.6 jit_solution(9704983205362102717)
XLA Ops:
  0.6 149.8 %conditional.1 = (bf16[3,64,4096]{2,1,0:T(8,128)(2,1)}, bf16[1,64,4096]{2,1,0:T(8,128)(2,1)}, f32[1,2,2,128]{3,2,1,0:T(2,128)}) conditional(s32[]{:T(128)} %convert_element_type.3, (bf16[3,64,4096]{2,1,0:T(8,128)(2,1)}, bf16[3,64,4096]{2,1,0:T(8,128)(2,1)}, bf16[1,64,4096]{2,1,0:T(8,128)(2,1)}, f32[4,2,32,128]{3,2,1,0:T(8,128)}, s32[8,128]{1,0:T(8,128)}, ...), branch_computations={%region_0.0_spmd, %region_2.0_spmd} | conditional | flops 2147485184 | bytes 31539674 | solution.py:491
  0.7 3.9 %pack.5 = bf16[16,14,64,128]{3,2,1,0:T(8,128)(2,1)} custom-call(bf16[3,64,4096]{2,1,0:T(8,128)(2,1)} %get-tuple-element.43.refs_0_, bf16[1,64,4096]{2,1,0:T(8,128)(2,1)} %get-tuple-element.44.refs_1_, bf16[3,64,4096]{2,1,0:T(8,128)(2,1)} %get-tuple-element.45.refs_2_), custom_call_target="tpu_custom_call" | custom-call | tf_op jit(solution)/shard_map/cond/branch_1_fun/pack/pallas_call | solution.py:300
  4.6 0.0 copy-start.6
  4.6 9.7 %all-to-all-start.3 = ((bf16[16,14,64,128]{3,2,1,0:T(8,128)(2,1)}), bf16[16,14,64,128]{3,2,1,0:T(8,128)(2,1)}, u32[]{:S(2)}, u32[]{:S(2)}) async-start(bf16[16,14,64,128]{3,2,1,0:T(8,128)(2,1)} %pack.5), calls=%async_computation.3 | async-start | bytes 7340032 | tf_op jit(solution)/shard_map/cond/branch_1_fun/all_to_all | solution.py:395
  14.3 0.7 constant_dynamic-slice_fusion.2
  15.0 68.7 %all-to-all-done.3.group_ref = bf16[16,14,64,128]{3,2,1,0:T(8,128)(2,1)} async-done(((bf16[16,14,64,128]{3,2,1,0:T(8,128)(2,1)}), bf16[16,14,64,128]{3,2,1,0:T(8,128)(2,1)}, u32[]{:S(2)}, u32[]{:S(2)}) %all-to-all-start.3) | async-done | bytes 3670048 | tf_op jit(solution)/shard_map/cond/branch_1_fun/all_to_all | solution.py:395
  83.7 0.0 copy-done.6
  83.7 9.4 %backward.3 = (bf16[16,6,64,128]{3,2,1,0:T(8,128)(2,1)}, f32[2,2,1,128]{3,2,1,0:T(1,128)S(1)}) custom-call(bf16[16,14,64,128]{3,2,1,0:T(8,128)(2,1)} %all-to-all-done.3.group_ref, f32[2,2,1,128]{3,2,1,0:T(1,128)S(1)} %bitcast.33, s32[8,128]{1,0:T(8,128)S(1)} %copy-done.6), custom_call_target="tpu_custom_call" | custom-call | flops 1610612736 | bytes 3670016 | tf_op jit(solution)/shard_map/cond/branch_1_fun/backward/pallas_call | solution.py:377
  93.1 0.0 copy-start.4
  93.1 0.0 copy-start.2
  93.1 3.7 %all-to-all-start.4 = ((bf16[16,6,64,128]{3,2,1,0:T(8,128)(2,1)}), bf16[16,6,64,128]{3,2,1,0:T(8,128)(2,1)S(1)}, u32[]{:S(2)}, u32[]{:S(2)}) async-start(bf16[16,6,64,128]{3,2,1,0:T(8,128)(2,1)} %get-tuple-element.49), calls=%async_computation.4 | async-start | bytes 3145728 | tf_op jit(solution)/shard_map/cond/branch_1_fun/all_to_all | solution.py:395
  96.8 0.0 copy-done.4
  96.9 3.7 %collective-permute-start.1 = (f32[2,2,128]{2,1,0:T(2,128)S(1)}, f32[2,2,128]{2,1,0:T(2,128)S(1)}, u32[]{:S(2)}, u32[]{:S(2)}) collective-permute-start(f32[2,2,128]{2,1,0:T(2,128)S(1)} %bitcast_add_fusion.2), channel_id=1, source_target_pairs={{0,192},{192,0},{1,193},{193,1},{2,194},{194,2},{3,195},{195,3},{4... | collective-permute-start | bytes 6152 | tf_op jit(solution)/shard_map/cond/branch_1_fun/ppermute | solution.py:459
  100.6 0.0 copy-done.2
  100.6 4.7 %forward.3 = bf16[16,2,64,128]{3,2,1,0:T(8,128)(2,1)} custom-call(bf16[16,14,64,128]{3,2,1,0:T(8,128)(2,1)} %all-to-all-done.3.group_ref, f32[2,2,1,128]{3,2,1,0:T(1,128)S(1)} %bitcast.30, s32[8,128]{1,0:T(8,128)S(1)} %copy-done.2), custom_call_target="tpu_custom_call" | custom-call | flops 536870912 | bytes 2097152 | tf_op jit(solution)/shard_map/cond/branch_1_fun/forward/pallas_call | solution.py:377
  105.3 0.0 collective-permute-done.1
  105.3 9.2 %psum.13.in_ref = f32[2,2,128]{2,1,0:T(2,128)} all-reduce(f32[2,2,128]{2,1,0:T(2,128)S(1)} %bitcast_add_fusion.3), channel_id=1, replica_groups=mesh['pipe'=4,'head'=16,'dp'=4] {'dp'}, use_global_device_ids=true, to_apply=%region_3.0 | all-reduce | flops 512 | bytes 4096 | tf_op jit(solution)/shard_map/cond/branch_1_fun/psum | solution.py:460
  114.5 14.9 %all-to-all-done.4.in_ref = bf16[16,6,64,128]{3,2,1,0:T(8,128)(2,1)S(1)} async-done(((bf16[16,6,64,128]{3,2,1,0:T(8,128)(2,1)}), bf16[16,6,64,128]{3,2,1,0:T(8,128)(2,1)S(1)}, u32[]{:S(2)}, u32[]{:S(2)}) %all-to-all-start.4) | async-done | bytes 1572896 | tf_op jit(solution)/shard_map/cond/branch_1_fun/all_to_all | solution.py:395
  129.4 5.7 %all-to-all-start.5 = ((bf16[16,2,64,128]{3,2,1,0:T(8,128)(2,1)}), bf16[16,2,64,128]{3,2,1,0:T(8,128)(2,1)S(1)}, u32[]{:S(2)}, u32[]{:S(2)}) async-start(bf16[16,2,64,128]{3,2,1,0:T(8,128)(2,1)} %forward.3), calls=%async_computation.5 | async-start | bytes 1048576 | tf_op jit(solution)/shard_map/cond/branch_1_fun/all_to_all | solution.py:395
  135.1 1.3 settle.3
  136.4 1.4 unpack.4
  137.8 11.4 %all-to-all-done.5.in_ref = bf16[16,2,64,128]{3,2,1,0:T(8,128)(2,1)S(1)} async-done(((bf16[16,2,64,128]{3,2,1,0:T(8,128)(2,1)}), bf16[16,2,64,128]{3,2,1,0:T(8,128)(2,1)S(1)}, u32[]{:S(2)}, u32[]{:S(2)}) %all-to-all-start.5) | async-done | bytes 524320 | tf_op jit(solution)/shard_map/cond/branch_1_fun/all_to_all | solution.py:395
  149.2 1.1 unpack.5
  (2 shorter events, 0.0 us)
Async XLA Ops:
  4.6 79.1 %copy-start.6 = (s32[8,128]{1,0:T(8,128)S(1)}, s32[8,128]{1,0:T(8,128)}, u32[]{:S(2)}) copy-start(s32[8,128]{1,0:T(8,128)} %get-tuple-element.47.doc_ref) | copy-start | bytes 12292 | tf_op jit(solution)/shard_map/cond
  4.6 79.1 %all-to-all-start.3 = ((bf16[16,14,64,128]{3,2,1,0:T(8,128)(2,1)}), bf16[16,14,64,128]{3,2,1,0:T(8,128)(2,1)}, u32[]{:S(2)}, u32[]{:S(2)}) async-start(bf16[16,14,64,128]{3,2,1,0:T(8,128)(2,1)} %pack.5), calls=%async_computation.3 | async-start | bytes 7340032 | tf_op jit(solution)/shard_map/cond/branch_1_fun/all_to_all | solution.py:395
  93.1 3.8 %copy-start.4 = (f32[2,2,2,128]{3,2,1,0:T(2,128)S(1)}, f32[2,2,2,128]{3,2,1,0:T(2,128)}, u32[]{:S(2)}) copy-start(f32[2,2,2,128]{3,2,1,0:T(2,128)} %get-tuple-element.52) | copy-start | bytes 12292 | tf_op jit(solution)/shard_map/cond
  93.1 7.5 %copy-start.2 = (s32[8,128]{1,0:T(8,128)S(1)}, s32[8,128]{1,0:T(8,128)}, u32[]{:S(2)}) copy-start(s32[8,128]{1,0:T(8,128)} %get-tuple-element.51.doc_ref) | copy-start | bytes 12292 | tf_op jit(solution)/shard_map/cond
  93.1 36.3 %all-to-all-start.4 = ((bf16[16,6,64,128]{3,2,1,0:T(8,128)(2,1)}), bf16[16,6,64,128]{3,2,1,0:T(8,128)(2,1)S(1)}, u32[]{:S(2)}, u32[]{:S(2)}) async-start(bf16[16,6,64,128]{3,2,1,0:T(8,128)(2,1)} %get-tuple-element.49), calls=%async_computation.4 | async-start | bytes 3145728 | tf_op jit(solution)/shard_map/cond/branch_1_fun/all_to_all | solution.py:395
  96.9 8.5 %collective-permute-start.1 = (f32[2,2,128]{2,1,0:T(2,128)S(1)}, f32[2,2,128]{2,1,0:T(2,128)S(1)}, u32[]{:S(2)}, u32[]{:S(2)}) collective-permute-start(f32[2,2,128]{2,1,0:T(2,128)S(1)} %bitcast_add_fusion.2), channel_id=1, source_target_pairs={{0,192},{192,0},{1,193},{193,1},{2,194},{194,2},{3,195},{195,3},{4... | collective-permute-start | bytes 6152 | tf_op jit(solution)/shard_map/cond/branch_1_fun/ppermute | solution.py:459
  129.4 19.7 %all-to-all-start.5 = ((bf16[16,2,64,128]{3,2,1,0:T(8,128)(2,1)}), bf16[16,2,64,128]{3,2,1,0:T(8,128)(2,1)S(1)}, u32[]{:S(2)}, u32[]{:S(2)}) async-start(bf16[16,2,64,128]{3,2,1,0:T(8,128)(2,1)} %forward.3), calls=%async_computation.5 | async-start | bytes 1048576 | tf_op jit(solution)/shard_map/cond/branch_1_fun/all_to_all | solution.py:395

commit v4 on v3

--- a/solution.py
+++ b/solution.py
@@ -10,7 +10,7 @@
 
 EPS = 1e-06
 LONGEST = 512
-BLOCK = 128
+BLOCK = 256
 NT = (((1,), (1,)), ((), ()))
 NN = (((1,), (0,)), ((), ()))
 F32 = jnp.float32
@@ -40,7 +40,7 @@
     return low, (block + 1) * BLOCK
 
 
-FORWARD_GROUP, BACKWARD_GROUP, KEY_GROUP = 8, 4, 4
+FORWARD_GROUP, BACKWARD_GROUP, KEY_GROUP = 4, 4, 4
 
 
 def groups_of(count, blocks, size):

time: 151 us -> 153 us (1.013)
  other arithmetic: 0.01 us -> 2.7 us
    unnamed x0 -> x2, other arithmetic: none -> 2.69 us
    all_to_all x3, starting transfers between devices: 19 us -> 20.7 us  [exchange(): lax.all_to_all(value, 'head', split_axis=0, concat_axis=0, tiled=True)]
where the time goes in v4:
time: 153 us
  waiting for transfers between devices  94.1 us (62%)
  starting transfers between devices  23.9 us (16%)
  Pallas kernels  20.5 us (13%)
  blocking collectives  9.17 us (6%)
  other arithmetic  2.7 us (2%)
    all_to_all x3, waiting for transfers between devices, exchange(): lax.all_to_all(value, 'head', split_axis=0, concat_axis=0, tiled=True)  94.1 us
    all_to_all x3, starting transfers between devices, exchange(): lax.all_to_all(value, 'head', split_axis=0, concat_axis=0, tiled=True)  20.7 us
    pallas_call x2, Pallas kernels, attend(): pl.pallas_call(functools.partial(forward_kernel if name == 'f' else backw...  12.9 us
    psum x1, blocking collectives, branch(): total = lax.psum(accum[0] + mirrored, 'dp')  9.17 us
    pallas_call x1, Pallas kernels, pack(): pl.pallas_call(functools.partial(pack_kernel, pieces, ranks), in_specs=[A...  3.93 us
    ppermute x1, starting transfers between devices, branch(): mirrored = lax.ppermute(up_local, 'pipe', mirror)  3.19 us
  transfers between devices with their start and end apart: 4, of which 3 were waited for; matrix products, arithmetic and copies ran while one was open for 0% of the time, Pallas kernels for 5%

profile of v4, /device:TPU:2, one launch (start us, length us, event | category | flops | bytes accessed | tf_op | source)
XLA Modules:
  0.0 152.8 jit_solution(6098237865062489848)
XLA Ops:
  0.6 0.5 broadcast.6
  1.2 1.3 reduce.7
  2.5 1.3 reduce.6
  3.9 148.8 %conditional.1 = (bf16[3,64,4096]{2,1,0:T(8,128)(2,1)}, bf16[1,64,4096]{2,1,0:T(8,128)(2,1)}, f32[1,2,2,128]{3,2,1,0:T(2,128)}) conditional(s32[]{:T(128)} %convert_element_type.3, (bf16[3,64,4096]{2,1,0:T(8,128)(2,1)}, bf16[3,64,4096]{2,1,0:T(8,128)(2,1)}, bf16[1,64,4096]{2,1,0:T(8,128)(2,1)}, f32[4,2,32,128]{3,2,1,0:T(8,128)}, ...), branch_computations={%region_0.0_spmd, %region_2.0_spmd} | conditional | flops 2147485184 | bytes 31506850 | solution.py:491
  3.9 3.9 %pack.5 = bf16[16,14,64,128]{3,2,1,0:T(8,128)(2,1)} custom-call(bf16[3,64,4096]{2,1,0:T(8,128)(2,1)} %get-tuple-element.43.refs_0_, bf16[1,64,4096]{2,1,0:T(8,128)(2,1)} %get-tuple-element.44.refs_1_, bf16[3,64,4096]{2,1,0:T(8,128)(2,1)} %get-tuple-element.45.refs_2_), custom_call_target="tpu_custom_call" | custom-call | tf_op jit(solution)/shard_map/cond/branch_1_fun/pack/pallas_call | solution.py:300
  7.8 9.7 %all-to-all-start.3 = ((bf16[16,14,64,128]{3,2,1,0:T(8,128)(2,1)}), bf16[16,14,64,128]{3,2,1,0:T(8,128)(2,1)}, u32[]{:S(2)}, u32[]{:S(2)}) async-start(bf16[16,14,64,128]{3,2,1,0:T(8,128)(2,1)} %pack.5), calls=%async_computation.3 | async-start | bytes 7340032 | tf_op jit(solution)/shard_map/cond/branch_1_fun/all_to_all | solution.py:395
  17.5 0.7 constant_dynamic-slice_fusion.2
  18.2 68.7 %all-to-all-done.3.group_ref = bf16[16,14,64,128]{3,2,1,0:T(8,128)(2,1)} async-done(((bf16[16,14,64,128]{3,2,1,0:T(8,128)(2,1)}), bf16[16,14,64,128]{3,2,1,0:T(8,128)(2,1)}, u32[]{:S(2)}, u32[]{:S(2)}) %all-to-all-start.3) | async-done | bytes 3670048 | tf_op jit(solution)/shard_map/cond/branch_1_fun/all_to_all | solution.py:395
  86.9 8.2 %backward.3 = (bf16[16,6,64,128]{3,2,1,0:T(8,128)(2,1)}, f32[2,2,1,128]{3,2,1,0:T(1,128)S(1)}) custom-call(bf16[16,14,64,128]{3,2,1,0:T(8,128)(2,1)} %all-to-all-done.3.group_ref, f32[2,2,1,128]{3,2,1,0:T(1,128)S(1)} %bitcast.31, s32[4,256]{1,0:T(4,128)S(1)} %get-tuple-element.47.doc_ref), custom_call_target="tpu_custom_call" | custom-call | flops 1610612736 | bytes 3670016 | tf_op jit(solution)/shard_map/cond/branch_1_fun/backward/pallas_call | solution.py:377
  95.1 0.0 copy-start.2
  95.1 3.7 %all-to-all-start.4 = ((bf16[16,6,64,128]{3,2,1,0:T(8,128)(2,1)}), bf16[16,6,64,128]{3,2,1,0:T(8,128)(2,1)S(1)}, u32[]{:S(2)}, u32[]{:S(2)}) async-start(bf16[16,6,64,128]{3,2,1,0:T(8,128)(2,1)} %get-tuple-element.49), calls=%async_computation.4 | async-start | bytes 3145728 | tf_op jit(solution)/shard_map/cond/branch_1_fun/all_to_all | solution.py:395
  98.8 0.0 copy-done.2
  98.8 3.2 %collective-permute-start.1 = (f32[2,2,128]{2,1,0:T(2,128)S(1)}, f32[2,2,128]{2,1,0:T(2,128)S(1)}, u32[]{:S(2)}, u32[]{:S(2)}) collective-permute-start(f32[2,2,128]{2,1,0:T(2,128)S(1)} %bitcast_add_fusion.2), channel_id=1, source_target_pairs={{0,192},{192,0},{1,193},{193,1},{2,194},{194,2},{3,195},{195,3},{4... | collective-permute-start | bytes 6152 | tf_op jit(solution)/shard_map/cond/branch_1_fun/ppermute | solution.py:459
  102.0 4.7 %forward.3 = bf16[16,2,64,128]{3,2,1,0:T(8,128)(2,1)} custom-call(bf16[16,14,64,128]{3,2,1,0:T(8,128)(2,1)} %all-to-all-done.3.group_ref, f32[2,2,1,128]{3,2,1,0:T(1,128)S(1)} %bitcast.28, s32[4,256]{1,0:T(4,128)S(1)} %get-tuple-element.51.doc_ref), custom_call_target="tpu_custom_call" | custom-call | flops 536870912 | bytes 2097152 | tf_op jit(solution)/shard_map/cond/branch_1_fun/forward/pallas_call | solution.py:377
  106.8 0.0 collective-permute-done.1
  106.8 9.2 %psum.13.in_ref = f32[2,2,128]{2,1,0:T(2,128)} all-reduce(f32[2,2,128]{2,1,0:T(2,128)S(1)} %bitcast_add_fusion.3), channel_id=1, replica_groups=mesh['pipe'=4,'head'=16,'dp'=4] {'dp'}, use_global_device_ids=true, to_apply=%region_3.0 | all-reduce | flops 512 | bytes 4096 | tf_op jit(solution)/shard_map/cond/branch_1_fun/psum | solution.py:460
  116.0 12.8 %all-to-all-done.4.in_ref = bf16[16,6,64,128]{3,2,1,0:T(8,128)(2,1)S(1)} async-done(((bf16[16,6,64,128]{3,2,1,0:T(8,128)(2,1)}), bf16[16,6,64,128]{3,2,1,0:T(8,128)(2,1)S(1)}, u32[]{:S(2)}, u32[]{:S(2)}) %all-to-all-start.4) | async-done | bytes 1572896 | tf_op jit(solution)/shard_map/cond/branch_1_fun/all_to_all | solution.py:395
  128.8 7.3 %all-to-all-start.5 = ((bf16[16,2,64,128]{3,2,1,0:T(8,128)(2,1)}), bf16[16,2,64,128]{3,2,1,0:T(8,128)(2,1)S(1)}, u32[]{:S(2)}, u32[]{:S(2)}) async-start(bf16[16,2,64,128]{3,2,1,0:T(8,128)(2,1)} %forward.3), calls=%async_computation.5 | async-start | bytes 1048576 | tf_op jit(solution)/shard_map/cond/branch_1_fun/all_to_all | solution.py:395
  136.1 1.2 settle.3
  137.3 1.4 unpack.4
  138.7 12.6 %all-to-all-done.5.in_ref = bf16[16,2,64,128]{3,2,1,0:T(8,128)(2,1)S(1)} async-done(((bf16[16,2,64,128]{3,2,1,0:T(8,128)(2,1)}), bf16[16,2,64,128]{3,2,1,0:T(8,128)(2,1)S(1)}, u32[]{:S(2)}, u32[]{:S(2)}) %all-to-all-start.5) | async-done | bytes 524320 | tf_op jit(solution)/shard_map/cond/branch_1_fun/all_to_all | solution.py:395
  151.4 1.1 unpack.5
  (4 shorter events, 0.0 us)
Async XLA Ops:
  7.8 79.1 %all-to-all-start.3 = ((bf16[16,14,64,128]{3,2,1,0:T(8,128)(2,1)}), bf16[16,14,64,128]{3,2,1,0:T(8,128)(2,1)}, u32[]{:S(2)}, u32[]{:S(2)}) async-start(bf16[16,14,64,128]{3,2,1,0:T(8,128)(2,1)} %pack.5), calls=%async_computation.3 | async-start | bytes 7340032 | tf_op jit(solution)/shard_map/cond/branch_1_fun/all_to_all | solution.py:395
  95.1 3.7 %copy-start.2 = (f32[2,2,2,128]{3,2,1,0:T(2,128)S(1)}, f32[2,2,2,128]{3,2,1,0:T(2,128)}, u32[]{:S(2)}) copy-start(f32[2,2,2,128]{3,2,1,0:T(2,128)} %get-tuple-element.52) | copy-start | bytes 12292 | tf_op jit(solution)/shard_map/cond
  95.1 33.7 %all-to-all-start.4 = ((bf16[16,6,64,128]{3,2,1,0:T(8,128)(2,1)}), bf16[16,6,64,128]{3,2,1,0:T(8,128)(2,1)S(1)}, u32[]{:S(2)}, u32[]{:S(2)}) async-start(bf16[16,6,64,128]{3,2,1,0:T(8,128)(2,1)} %get-tuple-element.49), calls=%async_computation.4 | async-start | bytes 3145728 | tf_op jit(solution)/shard_map/cond/branch_1_fun/all_to_all | solution.py:395
  98.8 7.9 %collective-permute-start.1 = (f32[2,2,128]{2,1,0:T(2,128)S(1)}, f32[2,2,128]{2,1,0:T(2,128)S(1)}, u32[]{:S(2)}, u32[]{:S(2)}) collective-permute-start(f32[2,2,128]{2,1,0:T(2,128)S(1)} %bitcast_add_fusion.2), channel_id=1, source_target_pairs={{0,192},{192,0},{1,193},{193,1},{2,194},{194,2},{3,195},{195,3},{4... | collective-permute-start | bytes 6152 | tf_op jit(solution)/shard_map/cond/branch_1_fun/ppermute | solution.py:459
  128.8 22.6 %all-to-all-start.5 = ((bf16[16,2,64,128]{3,2,1,0:T(8,128)(2,1)}), bf16[16,2,64,128]{3,2,1,0:T(8,128)(2,1)S(1)}, u32[]{:S(2)}, u32[]{:S(2)}) async-start(bf16[16,2,64,128]{3,2,1,0:T(8,128)(2,1)} %forward.3), calls=%async_computation.5 | async-start | bytes 1048576 | tf_op jit(solution)/shard_map/cond/branch_1_fun/all_to_all | solution.py:395

commit v5 on v4

--- a/solution.py
+++ b/solution.py
@@ -11,6 +11,7 @@
 EPS = 1e-06
 LONGEST = 512
 BLOCK = 256
+LANES = 128
 NT = (((1,), (1,)), ((), ()))
 NN = (((1,), (0,)), ((), ()))
 F32 = jnp.float32
@@ -33,6 +34,11 @@
         count = jnp.sum((docs == value).astype(jnp.int32))
         first = first + jnp.where(docs > value, count, 0)
     return first
+
+
+def starts_at(starts, block):
+    per = BLOCK // LANES
+    return jnp.concatenate([starts[at : at + 1] for at in range(block * per, (block + 1) * per)], axis=1)
 
 
 def window(block):
@@ -117,7 +123,7 @@
             dot(key_ref[slot, low:high], query_ref[slot, block * BLOCK : high], NT)
             for (slot, block), (low, high) in zip(items, spans)
         ]
-        probs = probs_of(scores, [starts[block : block + 1] for _, block in items], spans, dim)
+        probs = probs_of(scores, [starts_at(starts, block) for _, block in items], spans, dim)
         probs = [jnp.concatenate([piece.astype(BF16) for piece in every], axis=0) for every in probs]
         results = [
             dot(value_t_ref[slot, :, low:high], prob)
@@ -176,7 +182,7 @@
             dot(part(slot, 2, low, high), part(slot, 3, here.start, here.stop), NT)
             for slot, low, high, here in every
         ]
-        probs = probs_of(scores, [starts[block : block + 1] for _, block in items], spans, dim)
+        probs = probs_of(scores, [starts_at(starts, block) for _, block in items], spans, dim)
         rounded = [jnp.concatenate([piece.astype(BF16) for piece in some], axis=0) for some in probs]
         results = [
             dot(value_t_refs[slot, :, low:high], some)
@@ -479,8 +485,8 @@
         bwd_qkv.reshape(tokens, 3, width).transpose(1, 0, 2),
         bwd_grad_out.reshape(1, tokens, width),
         norm_gain,
-        fwd_doc.reshape(-1, BLOCK),
-        bwd_doc.reshape(-1, BLOCK),
+        fwd_doc.reshape(-1, LANES),
+        bwd_doc.reshape(-1, LANES),
         grad_acc.reshape(2, 2, local_heads, dim),
     )
     plans = [(at ^ (at >> 1)) & 1 for at in range(pipe_count)]

time: 153 us -> 150 us (0.980)
  other arithmetic: 2.7 us -> 0.01 us
    unnamed x2 -> x0, other arithmetic: 2.69 us -> none
where the time goes in v5:
time: 150 us
  waiting for transfers between devices  93.2 us (62%)
  starting transfers between devices  24.8 us (17%)
  Pallas kernels  20.5 us (14%)
  blocking collectives  9.19 us (6%)
    all_to_all x3, waiting for transfers between devices, exchange(): lax.all_to_all(value, 'head', split_axis=0, concat_axis=0, tiled=True)  93.2 us
    all_to_all x3, starting transfers between devices, exchange(): lax.all_to_all(value, 'head', split_axis=0, concat_axis=0, tiled=True)  21.1 us
    pallas_call x2, Pallas kernels, attend(): pl.pallas_call(functools.partial(forward_kernel if name == 'f' else backw...  12.9 us
    psum x1, blocking collectives, branch(): total = lax.psum(accum[0] + mirrored, 'dp')  9.19 us
    pallas_call x1, Pallas kernels, pack(): pl.pallas_call(functools.partial(pack_kernel, pieces, ranks), in_specs=[A...  3.91 us
    ppermute x1, starting transfers between devices, branch(): mirrored = lax.ppermute(up_local, 'pipe', mirror)  3.69 us
  transfers between devices with their start and end apart: 4, of which 3 were waited for; matrix products, arithmetic and copies ran while one was open for 0% of the time, Pallas kernels for 5%

profile of v5, /device:TPU:2, one launch (start us, length us, event | category | flops | bytes accessed | tf_op | source)
XLA Modules:
  0.0 149.7 jit_solution(9595834175701132419)
XLA Ops:
  0.6 148.9 %conditional.1 = (bf16[3,64,4096]{2,1,0:T(8,128)(2,1)}, bf16[1,64,4096]{2,1,0:T(8,128)(2,1)}, f32[1,2,2,128]{3,2,1,0:T(2,128)}) conditional(s32[]{:T(128)} %convert_element_type.3, (bf16[3,64,4096]{2,1,0:T(8,128)(2,1)}, bf16[3,64,4096]{2,1,0:T(8,128)(2,1)}, bf16[1,64,4096]{2,1,0:T(8,128)(2,1)}, f32[4,2,32,128]{3,2,1,0:T(8,128)}, s32[8,128]{1,0:T(8,128)}, ...), branch_computations={%region_0.0_spmd, %region_2.0_spmd} | conditional | flops 2147485184 | bytes 31539674 | solution.py:497
  0.7 3.9 %pack.5 = bf16[16,14,64,128]{3,2,1,0:T(8,128)(2,1)} custom-call(bf16[3,64,4096]{2,1,0:T(8,128)(2,1)} %get-tuple-element.43.refs_0_, bf16[1,64,4096]{2,1,0:T(8,128)(2,1)} %get-tuple-element.44.refs_1_, bf16[3,64,4096]{2,1,0:T(8,128)(2,1)} %get-tuple-element.45.refs_2_), custom_call_target="tpu_custom_call" | custom-call | tf_op jit(solution)/shard_map/cond/branch_1_fun/pack/pallas_call | solution.py:306
  4.6 0.0 copy-start.6
  4.6 9.7 %all-to-all-start.3 = ((bf16[16,14,64,128]{3,2,1,0:T(8,128)(2,1)}), bf16[16,14,64,128]{3,2,1,0:T(8,128)(2,1)}, u32[]{:S(2)}, u32[]{:S(2)}) async-start(bf16[16,14,64,128]{3,2,1,0:T(8,128)(2,1)} %pack.5), calls=%async_computation.3 | async-start | bytes 7340032 | tf_op jit(solution)/shard_map/cond/branch_1_fun/all_to_all | solution.py:401
  14.3 0.7 constant_dynamic-slice_fusion.2
  15.0 68.7 %all-to-all-done.3.group_ref = bf16[16,14,64,128]{3,2,1,0:T(8,128)(2,1)} async-done(((bf16[16,14,64,128]{3,2,1,0:T(8,128)(2,1)}), bf16[16,14,64,128]{3,2,1,0:T(8,128)(2,1)}, u32[]{:S(2)}, u32[]{:S(2)}) %all-to-all-start.3) | async-done | bytes 3670048 | tf_op jit(solution)/shard_map/cond/branch_1_fun/all_to_all | solution.py:401
  83.7 0.0 copy-done.6
  83.7 8.2 %backward.3 = (bf16[16,6,64,128]{3,2,1,0:T(8,128)(2,1)}, f32[2,2,1,128]{3,2,1,0:T(1,128)S(1)}) custom-call(bf16[16,14,64,128]{3,2,1,0:T(8,128)(2,1)} %all-to-all-done.3.group_ref, f32[2,2,1,128]{3,2,1,0:T(1,128)S(1)} %bitcast.33, s32[8,128]{1,0:T(8,128)S(1)} %copy-done.6), custom_call_target="tpu_custom_call" | custom-call | flops 1610612736 | bytes 3670016 | tf_op jit(solution)/shard_map/cond/branch_1_fun/backward/pallas_call | solution.py:383
  91.9 0.0 copy-start.4
  92.0 0.0 copy-start.2
  92.0 3.7 %all-to-all-start.4 = ((bf16[16,6,64,128]{3,2,1,0:T(8,128)(2,1)}), bf16[16,6,64,128]{3,2,1,0:T(8,128)(2,1)S(1)}, u32[]{:S(2)}, u32[]{:S(2)}) async-start(bf16[16,6,64,128]{3,2,1,0:T(8,128)(2,1)} %get-tuple-element.49), calls=%async_computation.4 | async-start | bytes 3145728 | tf_op jit(solution)/shard_map/cond/branch_1_fun/all_to_all | solution.py:401
  95.7 0.0 copy-done.4
  95.7 3.7 %collective-permute-start.1 = (f32[2,2,128]{2,1,0:T(2,128)S(1)}, f32[2,2,128]{2,1,0:T(2,128)S(1)}, u32[]{:S(2)}, u32[]{:S(2)}) collective-permute-start(f32[2,2,128]{2,1,0:T(2,128)S(1)} %bitcast_add_fusion.2), channel_id=1, source_target_pairs={{0,192},{192,0},{1,193},{193,1},{2,194},{194,2},{3,195},{195,3},{4... | collective-permute-start | bytes 6152 | tf_op jit(solution)/shard_map/cond/branch_1_fun/ppermute | solution.py:465
  99.4 0.0 copy-done.2
  99.4 4.7 %forward.3 = bf16[16,2,64,128]{3,2,1,0:T(8,128)(2,1)} custom-call(bf16[16,14,64,128]{3,2,1,0:T(8,128)(2,1)} %all-to-all-done.3.group_ref, f32[2,2,1,128]{3,2,1,0:T(1,128)S(1)} %bitcast.30, s32[8,128]{1,0:T(8,128)S(1)} %copy-done.2), custom_call_target="tpu_custom_call" | custom-call | flops 536870912 | bytes 2097152 | tf_op jit(solution)/shard_map/cond/branch_1_fun/forward/pallas_call | solution.py:383
  104.1 0.0 collective-permute-done.1
  104.2 9.2 %psum.13.in_ref = f32[2,2,128]{2,1,0:T(2,128)} all-reduce(f32[2,2,128]{2,1,0:T(2,128)S(1)} %bitcast_add_fusion.3), channel_id=1, replica_groups=mesh['pipe'=4,'head'=16,'dp'=4] {'dp'}, use_global_device_ids=true, to_apply=%region_3.0 | all-reduce | flops 512 | bytes 4096 | tf_op jit(solution)/shard_map/cond/branch_1_fun/psum | solution.py:466
  113.3 11.9 %all-to-all-done.4.in_ref = bf16[16,6,64,128]{3,2,1,0:T(8,128)(2,1)S(1)} async-done(((bf16[16,6,64,128]{3,2,1,0:T(8,128)(2,1)}), bf16[16,6,64,128]{3,2,1,0:T(8,128)(2,1)S(1)}, u32[]{:S(2)}, u32[]{:S(2)}) %all-to-all-start.4) | async-done | bytes 1572896 | tf_op jit(solution)/shard_map/cond/branch_1_fun/all_to_all | solution.py:401
  125.2 7.8 %all-to-all-start.5 = ((bf16[16,2,64,128]{3,2,1,0:T(8,128)(2,1)}), bf16[16,2,64,128]{3,2,1,0:T(8,128)(2,1)S(1)}, u32[]{:S(2)}, u32[]{:S(2)}) async-start(bf16[16,2,64,128]{3,2,1,0:T(8,128)(2,1)} %forward.3), calls=%async_computation.5 | async-start | bytes 1048576 | tf_op jit(solution)/shard_map/cond/branch_1_fun/all_to_all | solution.py:401
  133.0 1.3 settle.3
  134.2 1.4 unpack.4
  135.6 12.6 %all-to-all-done.5.in_ref = bf16[16,2,64,128]{3,2,1,0:T(8,128)(2,1)S(1)} async-done(((bf16[16,2,64,128]{3,2,1,0:T(8,128)(2,1)}), bf16[16,2,64,128]{3,2,1,0:T(8,128)(2,1)S(1)}, u32[]{:S(2)}, u32[]{:S(2)}) %all-to-all-start.5) | async-done | bytes 524320 | tf_op jit(solution)/shard_map/cond/branch_1_fun/all_to_all | solution.py:401
  148.3 1.1 unpack.5
  (2 shorter events, 0.0 us)
Async XLA Ops:
  4.6 79.1 %copy-start.6 = (s32[8,128]{1,0:T(8,128)S(1)}, s32[8,128]{1,0:T(8,128)}, u32[]{:S(2)}) copy-start(s32[8,128]{1,0:T(8,128)} %get-tuple-element.47.doc_ref) | copy-start | bytes 12292 | tf_op jit(solution)/shard_map/cond
  4.6 79.1 %all-to-all-start.3 = ((bf16[16,14,64,128]{3,2,1,0:T(8,128)(2,1)}), bf16[16,14,64,128]{3,2,1,0:T(8,128)(2,1)}, u32[]{:S(2)}, u32[]{:S(2)}) async-start(bf16[16,14,64,128]{3,2,1,0:T(8,128)(2,1)} %pack.5), calls=%async_computation.3 | async-start | bytes 7340032 | tf_op jit(solution)/shard_map/cond/branch_1_fun/all_to_all | solution.py:401
  91.9 3.8 %copy-start.4 = (f32[2,2,2,128]{3,2,1,0:T(2,128)S(1)}, f32[2,2,2,128]{3,2,1,0:T(2,128)}, u32[]{:S(2)}) copy-start(f32[2,2,2,128]{3,2,1,0:T(2,128)} %get-tuple-element.52) | copy-start | bytes 12292 | tf_op jit(solution)/shard_map/cond
  92.0 7.5 %copy-start.2 = (s32[8,128]{1,0:T(8,128)S(1)}, s32[8,128]{1,0:T(8,128)}, u32[]{:S(2)}) copy-start(s32[8,128]{1,0:T(8,128)} %get-tuple-element.51.doc_ref) | copy-start | bytes 12292 | tf_op jit(solution)/shard_map/cond
  92.0 33.2 %all-to-all-start.4 = ((bf16[16,6,64,128]{3,2,1,0:T(8,128)(2,1)}), bf16[16,6,64,128]{3,2,1,0:T(8,128)(2,1)S(1)}, u32[]{:S(2)}, u32[]{:S(2)}) async-start(bf16[16,6,64,128]{3,2,1,0:T(8,128)(2,1)} %get-tuple-element.49), calls=%async_computation.4 | async-start | bytes 3145728 | tf_op jit(solution)/shard_map/cond/branch_1_fun/all_to_all | solution.py:401
  95.7 8.4 %collective-permute-start.1 = (f32[2,2,128]{2,1,0:T(2,128)S(1)}, f32[2,2,128]{2,1,0:T(2,128)S(1)}, u32[]{:S(2)}, u32[]{:S(2)}) collective-permute-start(f32[2,2,128]{2,1,0:T(2,128)S(1)} %bitcast_add_fusion.2), channel_id=1, source_target_pairs={{0,192},{192,0},{1,193},{193,1},{2,194},{194,2},{3,195},{195,3},{4... | collective-permute-start | bytes 6152 | tf_op jit(solution)/shard_map/cond/branch_1_fun/ppermute | solution.py:465
  125.2 23.1 %all-to-all-start.5 = ((bf16[16,2,64,128]{3,2,1,0:T(8,128)(2,1)}), bf16[16,2,64,128]{3,2,1,0:T(8,128)(2,1)S(1)}, u32[]{:S(2)}, u32[]{:S(2)}) async-start(bf16[16,2,64,128]{3,2,1,0:T(8,128)(2,1)} %forward.3), calls=%async_computation.5 | async-start | bytes 1048576 | tf_op jit(solution)/shard_map/cond/branch_1_fun/all_to_all | solution.py:401
